TPU v7x, 512 devices: a whole 4x8x8 slice. The times are simulated.
512 devices in a mesh: member: 32 (over y, x), region: 16 (over z, core).
Axes of the slice: x: 4, y: 8, z: 8, core: 2. Of those that a mesh axis runs over, the one named last changes fastest.
Arguments:
- background_spread: bfloat16 [256, 512, 6, 128], P('member', 'region'), may hold values from -6 to 6
- sensed_anomalies: bfloat16 [256, 512, 128], P('member', 'region'), may hold values from -6 to 6
- misfit_vector: bfloat16 [512, 128], P('region'), may hold values from -6 to 6
- damped_precision: float32 [512, 4, 128], P('region'), may hold values from 0.05 to 1
- sensed_patch_table: int32 [512, 4], P('region'), may hold values from 0 to 37, as said below
- zone_patch_tally: int32 [16], P('region'), may hold values from 2 to 32, as said below
Outputs:
- analysis: bfloat16 [256, 512, 6, 128], P('member', 'region')
Inputs may be any that keep to these rules, and one draw needn't show every extreme that they name: `sensed_patch_table`: for each region the live slots' lists run across the region's observation blocks from the first to the last; the first live slot uses index 0 and the last live slot the largest index. `zone_patch_tally`: some region has all 32 slots live.
All inputs are finite; a program needn't handle non-finite values.
Results may differ from a plain program's by a relative error of at most 0.0034.
Values may be sent and summed in bfloat16 or wider, within the bound.
No kernel may reach another device: no remote copies, remote signals or barrier semaphores. Data moves between devices by JAX's collectives and lax.ppermute only.
A program may use at most 64 MiB of HBM per device.

v0:
```python
import jax
import jax.numpy as jnp
from jax import lax
from jax.sharding import PartitionSpec as P

HW = 3
NS_STEPS = 5


def with_halo(cells, sides, width):
    for axis, dim in sides:
        count = lax.axis_size(axis)
        head = lax.slice_in_dim(cells, 0, width, axis=dim)
        tail = lax.slice_in_dim(cells, cells.shape[dim] - width, cells.shape[dim], axis=dim)
        cells = jnp.concatenate(
            [
                lax.ppermute(tail, axis, [(i, (i + 1) % count) for i in range(count)]),
                cells,
                lax.ppermute(head, axis, [((i + 1) % count, i) for i in range(count)]),
            ],
            axis=dim,
        )
    return cells


def matmul_high(left, right):
    return jnp.einsum("bkj,bjl->bkl", left, right, precision=lax.Precision.HIGHEST)


def analyse(background_field, yb, loc, innov):
    sample_lines = background_field.shape[0]
    scaled = (yb.astype(jnp.float32) * loc[None]).astype(jnp.bfloat16)
    gram = jnp.einsum("kbp,jbp->bkj", scaled, yb, preferred_element_type=jnp.float32)
    drive = jnp.einsum("kbp,bp->bk", scaled, innov, preferred_element_type=jnp.float32)
    ident = jnp.eye(sample_lines, dtype=jnp.float32)[None]
    amat = ident + gram / jnp.float32(sample_lines - 1)
    frob = jnp.sqrt(jnp.sum(amat * amat, axis=(1, 2)))[:, None, None]
    upper = amat / frob
    lower = ident
    for step in range(NS_STEPS):
        middle = 1.5 * ident - 0.5 * matmul_high(lower, upper)
        upper = matmul_high(upper, middle)
        lower = matmul_high(middle, lower)
    trans = lower / jnp.sqrt(frob)
    inner = jnp.einsum("bkj,bj->bk", trans, drive, precision=lax.Precision.HIGHEST)
    wmean = jnp.einsum("bkj,bj->bk", trans, inner, precision=lax.Precision.HIGHEST) / jnp.float32(
        sample_lines - 1
    )
    weights = (trans + wmean[:, :, None]).astype(jnp.bfloat16)
    mean_state = jnp.mean(background_field.astype(jnp.float32), axis=0)
    mixed = jnp.einsum(
        "kbc,bkj->jbc", background_field, weights, preferred_element_type=jnp.float32
    )
    colsum = jnp.sum(weights.astype(jnp.float32), axis=1)
    return mean_state[None] + mixed - mean_state[None] * jnp.transpose(colsum)[:, :, None]


def one_hot_rows(indices, extent):
    return (indices.reshape(-1)[:, None] == jnp.arange(extent, dtype=jnp.int32)[None]).astype(
        jnp.bfloat16
    )


def shards(
    background_spread,
    sensed_anomalies,
    misfit_vector,
    damped_precision,
    sensed_patch_table,
    zone_patch_tally,
):
    local_members = sensed_anomalies.shape[0]
    zone_for_place = background_spread.shape[1]
    per_device = zone_for_place // lax.axis_size("member")
    hops = sensed_patch_table.shape[1]
    obs_width = sensed_anomalies.shape[2]
    stacked = jnp.concatenate([sensed_anomalies, misfit_vector[None]], axis=0)
    extended = with_halo(stacked, (("region", 1),), HW)
    extent = extended.shape[1]
    pert_ext = extended[:local_members]
    innov_ext = extended[local_members]
    mesh_cells = lax.all_to_all(
        background_spread, "member", split_axis=1, concat_axis=0, tiled=True
    )
    sample_lines = mesh_cells.shape[0]
    first_slot = lax.axis_index("member") * per_device
    mine = lax.dynamic_slice_in_dim(sensed_patch_table, first_slot, per_device, 0)
    pick_mine = one_hot_rows(mine, extent)
    every_member = lax.all_gather(pert_ext, "member", axis=0, tiled=True)
    chosen = jnp.einsum(
        "qe,keo->kqo", pick_mine, every_member, preferred_element_type=jnp.float32
    ).astype(jnp.bfloat16)
    yb = chosen.reshape(sample_lines, per_device, hops * obs_width)
    innov = jnp.dot(pick_mine, innov_ext, preferred_element_type=jnp.float32).astype(jnp.bfloat16)
    innov = innov.reshape(per_device, hops * obs_width)
    loc = lax.dynamic_slice_in_dim(damped_precision, first_slot, per_device, 0).reshape(
        per_device, hops * obs_width
    )
    background_field = mesh_cells.reshape(sample_lines, per_device, -1)
    live_total = jnp.clip(zone_patch_tally[0] - first_slot, 0, per_device)
    solved = analyse(background_field, yb, loc, innov).astype(jnp.bfloat16)
    live = jnp.arange(per_device, dtype=jnp.int32) < live_total
    updated_result = jnp.where(live[None, :, None], solved, background_field)
    updated_result = updated_result.reshape(mesh_cells.shape)
    return lax.all_to_all(updated_result, "member", split_axis=0, concat_axis=1, tiled=True)


def solution(mesh):
    return jax.shard_map(
        shards,
        mesh=mesh,
        in_specs=(
            P("member", "region", None, None),
            P("member", "region", None),
            P("region", None),
            P("region", None, None),
            P("region", None),
            P("region"),
        ),
        out_specs=P("member", "region", None, None),
        check_vma=False,
    )
```

profile of v0, /device:TPU:8, one launch (start us, length us, event | category | flops | bytes accessed | tf_op | source)
XLA Modules:
  0.0 142.4 jit_solution(16989645323290798052)
XLA Ops:
  6.5 0.0 copy-start
  6.5 0.0 all-gather.2.cloned.1.call-start
  6.5 0.8 pad_maximum_fusion.2
  7.4 0.0 collective-permute-start
  7.4 8.5 %collective-permute-start.1 = (bf16[9,3,128]{2,1,0:T(4,128)(2,1)S(1)}, bf16[9,3,128]{2,1,0:T(4,128)(2,1)S(1)}, u32[]{:S(2)}, u32[]{:S(2)}) collective-permute-start(bf16[9,3,128]{2,1,0:T(4,128)(2,1)S(1)} %get-tuple-element.6), channel_id=1, source_target_pairs={{1,0},{2,1},{3,2},{4,3},{5,4},{6,5},{7,6},{8,7},{9,8},{10,9},{11,1... | collective-permute-start | bytes 20744 | tf_op jit(solution)/shard_map/ppermute | solution.py:19
  15.9 1.3 collective-permute-done
  17.2 0.1 collective-permute-done.1
  17.2 0.9 pad_maximum_fusion
  18.2 0.6 copy.28
  18.8 0.0 all-gather.2.cloned.1.call-update
  18.8 2.0 %copy.27 = bf16[8,32,6,128]{3,0,2,1:T(8,128)(2,1)} copy(bf16[8,32,6,128]{3,1,2,0:T(8,128)(2,1)} %param.6) | data formatting | bytes 786432 | tf_op args[0]
  20.8 10.2 %all-to-all-start = ((bf16[8,32,6,128]{3,0,2,1:T(8,128)(2,1)}), bf16[8,32,6,128]{3,0,2,1:T(8,128)(2,1)S(1)}, u32[]{:S(2)}, u32[]{:S(2)}) async-start(bf16[8,32,6,128]{3,0,2,1:T(8,128)(2,1)} %copy.27), calls=%async_computation | async-start | bytes 786432 | tf_op jit(solution)/shard_map/all_to_all | solution.py:82
  31.6 0.9 dynamic-slice_reduce_fusion
  32.5 0.0 copy-done
  32.5 0.9 fusion.14
  33.4 9.9 %all-to-all-done = bf16[8,32,6,128]{3,0,2,1:T(8,128)(2,1)S(1)} async-done(((bf16[8,32,6,128]{3,0,2,1:T(8,128)(2,1)}), bf16[8,32,6,128]{3,0,2,1:T(8,128)(2,1)S(1)}, u32[]{:S(2)}, u32[]{:S(2)}) %all-to-all-start) | async-done | bytes 393248 | tf_op jit(solution)/shard_map/all_to_all | solution.py:82
  43.3 0.1 convert_reduce_fusion
  43.4 58.0 %all-gather.2.cloned.1.call-done = bf16[256,38,128]{2,0,1:T(8,128)(2,1)} async-done(((bf16[8,38,128]{2,0,1:T(8,128)(2,1)}), bf16[256,38,128]{2,0,1:T(8,128)(2,1)}) %all-gather.2.cloned.1.call-update) | async-done | bytes 2490384 | tf_op jit(solution)/shard_map/all_gather | solution.py:89
  101.4 3.2 %bitcast_convert_fusion = (f32[256,4,128]{2,1,0:T(4,128)S(1)}, bf16[256,128,4]{1,2,0:T(4,128)(2,1)S(1)}) fusion(s32[4]{0:T(128)S(1)} %dynamic-slice_reduce_fusion, bf16[256,38,128]{2,0,1:T(8,128)(2,1)} %all-gather.2.cloned.1.call-done), kind=kOutput, calls=%fused_computation.30 | convolution fusion | flops 10223768 | bytes 3276816 | tf_op jit(solution)/shard_map/qe,keo->kqo/dot_general | solution.py:90
  104.6 0.2 reshape.260
  104.8 0.9 multiply_reduce_fusion
  106.5 0.3 fusion.12
  106.8 0.4 fusion.20
  107.2 0.3 fusion.19
  107.4 0.4 fusion.11
  107.8 0.4 fusion.35
  108.2 0.4 fusion.34
  108.6 0.4 fusion.10
  109.0 0.4 fusion.37
  109.4 0.4 fusion.36
  109.8 0.4 fusion.9
  110.2 0.4 fusion.38
  110.5 0.4 fusion.39
  110.9 0.2 convolution_bitcast_fusion.1
  111.1 0.4 fusion.8
  111.5 0.4 convolution_divide_fusion
  111.9 0.3 convolution_bitcast_fusion
  112.2 0.3 fusion.40
  112.5 0.2 convert_reduce_fusion.1
  112.7 0.4 fusion.4
  113.1 0.2 copy.30
  113.3 0.3 copy.31
  113.6 21.0 %all_to_all.33 = bf16[256,1,6,128]{3,2,1,0:T(8,128)(2,1)S(1)} all-to-all(bf16[256,1,6,128]{3,2,1,0:T(8,128)(2,1)S(1)} %copy.31), channel_id=1, replica_groups=mesh['member'=32,'region'=16] {'member'}, dimensions={0} | all-to-all | bytes 786432 | tf_op jit(solution)/shard_map/all_to_all | solution.py:105
  134.6 1.0 copy.33
  (5 shorter events, 0.0 us)
Async XLA Ops:
  6.5 26.0 %copy-start = (f32[32,4,128]{2,1,0:T(4,128)S(1)}, f32[32,4,128]{2,1,0:T(4,128)}, u32[]{:S(2)}) copy-start(f32[32,4,128]{2,1,0:T(4,128)} %param.9) | copy-start | bytes 196612
  6.5 94.9 %all-gather.2.cloned.1.call-start = ((), (), s32[]{:S(2)}) async-start(), calls=%async_computation.2 | async-start | bytes 2568192 | tf_op jit(solution)/shard_map/all_gather | solution.py:89
  7.4 9.8 %collective-permute-start = (bf16[9,3,128]{2,1,0:T(4,128)(2,1)S(1)}, bf16[9,3,128]{2,1,0:T(4,128)(2,1)S(1)}, u32[]{:S(2)}, u32[]{:S(2)}) collective-permute-start(bf16[9,3,128]{2,1,0:T(4,128)(2,1)S(1)} %get-tuple-element.5), channel_id=1, source_target_pairs={{0,1},{1,2},{2,3},{3,4},{4,5},{5,6},{6,7},{7,8},{8,9},{9,10},{10,1... | collective-permute-start | bytes 20744 | tf_op jit(solution)/shard_map/ppermute | solution.py:17
  7.4 9.9 %collective-permute-start.1 = (bf16[9,3,128]{2,1,0:T(4,128)(2,1)S(1)}, bf16[9,3,128]{2,1,0:T(4,128)(2,1)S(1)}, u32[]{:S(2)}, u32[]{:S(2)}) collective-permute-start(bf16[9,3,128]{2,1,0:T(4,128)(2,1)S(1)} %get-tuple-element.6), channel_id=1, source_target_pairs={{1,0},{2,1},{3,2},{4,3},{5,4},{6,5},{7,6},{8,7},{9,8},{10,9},{11,1... | collective-permute-start | bytes 20744 | tf_op jit(solution)/shard_map/ppermute | solution.py:19
  20.8 22.5 %all-to-all-start = ((bf16[8,32,6,128]{3,0,2,1:T(8,128)(2,1)}), bf16[8,32,6,128]{3,0,2,1:T(8,128)(2,1)S(1)}, u32[]{:S(2)}, u32[]{:S(2)}) async-start(bf16[8,32,6,128]{3,0,2,1:T(8,128)(2,1)} %copy.27), calls=%async_computation | async-start | bytes 786432 | tf_op jit(solution)/shard_map/all_to_all | solution.py:82
Sparse Core Ops, SparseCore 0:
  18.9 82.4 all-gather.1
where the time goes:
time: 143 us; the launch traced here: 142 us
  waiting for transfers between devices  69.3 us (48%)
  blocking collectives  21 us (15%)
  starting transfers between devices  18.7 us (13%)
  between operations  15 us (10%)
  matrix products  11.3 us (8%)
  local copies, waits for them, and re-layouts  5.24 us (4%)
  other arithmetic  1.97 us (1%)
    all_gather x1, waiting for transfers between devices, shards(): every_member = lax.all_gather(pert_ext, 'member', axis=0, tiled=True)  58 us
    all_to_all x1, blocking collectives, shards(): lax.all_to_all(updated_result, 'member', split_axis=0, concat_axis=1, til...  21 us
    all_to_all x1, starting transfers between devices, shards(): lax.all_to_all(background_spread, 'member', split_axis=1, concat_axis=0,...  10.2 us
    all_to_all x1, waiting for transfers between devices, shards(): lax.all_to_all(background_spread, 'member', split_axis=1, concat_axis=0,...  9.91 us
    ppermute x1, starting transfers between devices, with_halo(): lax.ppermute(head, axis, [((i + 1) % count, i) for i in range(count)])  8.49 us
    dot_general x14, matrix products, matmul_high(): jnp.einsum('bkj,bjl->bkl', left, right, precision=lax.Precision.HIGHEST)  5.17 us
    dot_general x1, matrix products, shards(): jnp.einsum('qe,keo->kqo', pick_mine, every_member, preferred_element_type...  3.21 us
  transfers between devices with their start and end apart: 4, of which 4 were waited for; matrix products, arithmetic and copies ran while one was open for 3% of the time, Pallas kernels for 0%

commit v1 on v0

v1 whole, which is shorter than its diff:
```python
import jax
import jax.numpy as jnp
from jax import lax
from jax.sharding import PartitionSpec as P

HW = 3
NS_STEPS = 5


def with_halo(cells, axis, dim, width):
    count = lax.axis_size(axis)
    head = lax.slice_in_dim(cells, 0, width, axis=dim)
    tail = lax.slice_in_dim(cells, cells.shape[dim] - width, cells.shape[dim], axis=dim)
    return jnp.concatenate(
        [
            lax.ppermute(tail, axis, [(i, (i + 1) % count) for i in range(count)]),
            cells,
            lax.ppermute(head, axis, [((i + 1) % count, i) for i in range(count)]),
        ],
        axis=dim,
    )


def matmul_high(left, right):
    return jnp.dot(left, right, precision=lax.Precision.HIGHEST)


def analyse(field, yb, loc, innov):
    lines = field.shape[0]
    scaled = (yb.astype(jnp.float32) * loc[None]).astype(jnp.bfloat16)
    gram = jnp.einsum("kp,jp->kj", scaled, yb, preferred_element_type=jnp.float32)
    drive = jnp.einsum("kp,p->k", scaled, innov, preferred_element_type=jnp.float32)
    ident = jnp.eye(lines, dtype=jnp.float32)
    amat = ident + gram / jnp.float32(lines - 1)
    frob = jnp.sqrt(jnp.sum(amat * amat))
    upper = amat / frob
    lower = ident
    for step in range(NS_STEPS):
        if step == 0:
            middle = 1.5 * ident - 0.5 * upper
            lower = middle
        else:
            middle = 1.5 * ident - 0.5 * matmul_high(lower, upper)
            lower = matmul_high(middle, lower)
        if step + 1 < NS_STEPS:
            upper = matmul_high(upper, middle)
    trans = lower / jnp.sqrt(frob)
    inner = jnp.dot(trans, drive, precision=lax.Precision.HIGHEST)
    wmean = jnp.dot(trans, inner, precision=lax.Precision.HIGHEST) / jnp.float32(lines - 1)
    weights = (trans + wmean[:, None]).astype(jnp.bfloat16)
    mean_state = jnp.mean(field.astype(jnp.float32), axis=0)
    mixed = jnp.einsum("kc,kj->jc", field, weights, preferred_element_type=jnp.float32)
    colsum = jnp.sum(weights.astype(jnp.float32), axis=0)
    return mean_state[None] + mixed - mean_state[None] * colsum[:, None]


def one_hot_rows(indices, extent):
    return (indices.reshape(-1)[:, None] == jnp.arange(extent, dtype=jnp.int32)[None]).astype(
        jnp.bfloat16
    )


def shards(forecast, anomalies, misfit, precision, table, tally):
    members, slots, fields, cells = forecast.shape
    used = table.shape[1]
    obs = anomalies.shape[2]
    ranks = lax.axis_size("member")
    stacked = jnp.concatenate([anomalies, misfit[None]], axis=0)
    extended = with_halo(stacked, "region", 1, HW)
    extent = extended.shape[1]
    me = lax.axis_index("member")
    pick = one_hot_rows(table, extent)
    chosen = jnp.einsum(
        "qe,meo->qmo", pick, extended[:members], preferred_element_type=jnp.float32
    ).astype(jnp.bfloat16)
    chosen = chosen.reshape(slots, used, members, obs)
    outgoing = jnp.concatenate([jnp.transpose(forecast, (1, 2, 0, 3)), chosen], axis=1)
    incoming = lax.all_to_all(outgoing, "member", 0, 0, tiled=True)
    lines = ranks * members
    mine = jnp.transpose(incoming, (0, 2, 1, 3)).reshape(lines, -1)
    field = mine[:, : fields * cells]
    yb = mine[:, fields * cells :]
    pick_mine = lax.dynamic_slice_in_dim(pick, me * used, used, 0)
    innov = jnp.dot(pick_mine, extended[members], preferred_element_type=jnp.float32).astype(
        jnp.bfloat16
    )
    innov = innov.reshape(used * obs)
    loc = lax.dynamic_slice_in_dim(precision, me, 1, 0).reshape(used * obs)
    solved = analyse(field, yb, loc, innov).astype(jnp.bfloat16)
    result = jnp.where(me < tally[0], solved, field)
    back = jnp.transpose(result.reshape(ranks, members, fields, cells), (0, 2, 1, 3))
    back = lax.all_to_all(back, "member", 0, 0, tiled=True)
    return jnp.transpose(back, (2, 0, 1, 3))


def solution(mesh):
    return jax.shard_map(
        shards,
        mesh=mesh,
        in_specs=(
            P("member", "region", None, None),
            P("member", "region", None),
            P("region", None),
            P("region", None, None),
            P("region", None),
            P("region"),
        ),
        out_specs=P("member", "region", None, None),
        check_vma=False,
    )
```

time: 143 us -> 67 us (0.47)
  the two profiles are of different devices: /device:TPU:8 before, /device:TPU:193 now
where the time goes in v1:
time: 67 us; the launch traced here: 66.7 us
  waiting for transfers between devices  20 us (30%)
  blocking collectives  19.5 us (29%)
  starting transfers between devices  13.5 us (20%)
  matrix products  7.3 us (11%)
  local copies, waits for them, and re-layouts  2.67 us (4%)
  other arithmetic  2.02 us (3%)
  between operations  1.59 us (2%)
    all_to_all x1, blocking collectives, shards(): back = lax.all_to_all(back, 'member', 0, 0, tiled=True)  19.5 us
    all_to_all x1, waiting for transfers between devices, shards(): incoming = lax.all_to_all(outgoing, 'member', 0, 0, tiled=True)  17.3 us
    all_to_all x1, starting transfers between devices, shards(): incoming = lax.all_to_all(outgoing, 'member', 0, 0, tiled=True)  9.67 us
    dot_general x12, matrix products, matmul_high(): return jnp.dot(left, right, precision=lax.Precision.HIGHEST)  4.68 us
    ppermute x1, starting transfers between devices, with_halo(): lax.ppermute(tail, axis, [(i, (i + 1) % count) for i in range(count)])  3.88 us
    ppermute x1, waiting for transfers between devices, with_halo(): lax.ppermute(head, axis, [((i + 1) % count, i) for i in range(count)])  2.78 us
    unnamed x10, local copies, waits for them, and re-layouts  1.4 us
  transfers between devices with their start and end apart: 3, of which 2 were waited for; matrix products, arithmetic and copies ran while one was open for 3% of the time, Pallas kernels for 0%

profile of v1, /device:TPU:193, one launch (start us, length us, event | category | flops | bytes accessed | tf_op | source)
XLA Modules:
  0.0 66.7 jit_solution(18096688034055775108)
XLA Ops:
  0.0 0.0 copy-start
  0.0 0.8 %pad_maximum_fusion.3 = (bf16[9,3,128]{2,1,0:T(4,128)(2,1)S(1)}, bf16[9,3,128]{2,1,0:T(4,128)(2,1)S(1)}) fusion(bf16[1,32,128]{2,1,0:T(8,128)(2,1)} %bitcast.64, bf16[8,32,128]{2,1,0:T(8,128)(2,1)} %param.7), kind=kLoop, calls=%fused_computation.60 | loop fusion | flops 27648 | bytes 87552 | tf_op jit(solution)/shard_map/slice | solution.py:13
  0.8 0.0 copy-start.3
  0.8 3.9 %collective-permute-start = (bf16[9,3,128]{2,1,0:T(4,128)(2,1)S(1)}, bf16[9,3,128]{2,1,0:T(4,128)(2,1)S(1)}, u32[]{:S(2)}, u32[]{:S(2)}) collective-permute-start(bf16[9,3,128]{2,1,0:T(4,128)(2,1)S(1)} %get-tuple-element.5), channel_id=1, source_target_pairs={{0,1},{1,2},{2,3},{3,4},{4,5},{5,6},{6,7},{7,8},{8,9},{9,10},{10,1... | collective-permute-start | bytes 20744 | tf_op jit(solution)/shard_map/ppermute | solution.py:16
  4.7 0.0 collective-permute-start.1
  4.7 0.0 copy-done.3
  4.7 0.1 copy.27
  4.8 0.1 eq.28
  4.9 0.0 copy-start.1
  4.9 0.0 copy-start.2
  4.9 1.3 %copy.31 = bf16[8,32,6,128]{3,0,2,1:T(8,128)(2,1)S(1)} copy(bf16[8,32,6,128]{3,1,2,0:T(8,128)(2,1)} %param.6) | data formatting | bytes 786432 | tf_op args[0]
  6.2 0.0 collective-permute-done
  6.2 2.8 %collective-permute-done.1 = bf16[9,3,128]{2,1,0:T(4,128)(2,1)S(1)} collective-permute-done((bf16[9,3,128]{2,1,0:T(4,128)(2,1)S(1)}, bf16[9,3,128]{2,1,0:T(4,128)(2,1)S(1)}, u32[]{:S(2)}, u32[]{:S(2)}) %collective-permute-start.1) | collective-permute-done | bytes 6944 | tf_op jit(solution)/shard_map/ppermute | solution.py:18
  9.0 0.0 copy-done.1
  9.0 0.0 copy-done.2
  9.0 0.3 convolution_convert_fusion
  9.3 0.3 copy.28
  9.6 0.9 %pad_maximum_fusion = bf16[32,10,8,128]{3,2,1,0:T(8,128)(2,1)} fusion(bf16[32,4,8,128]{3,2,1,0:T(8,128)(2,1)S(1)} %copy.28, bf16[32,6,8,128]{3,2,1,0:T(8,128)(2,1)S(1)} %bitcast.62), kind=kLoop, calls=%fused_computation.22 | loop fusion | flops 327680 | bytes 1310720 | tf_op jit(solution)/shard_map/concatenate | solution.py:77
  10.5 9.7 %all-to-all-start = ((bf16[32,10,8,128]{3,2,1,0:T(8,128)(2,1)}), bf16[32,10,8,128]{3,2,1,0:T(8,128)(2,1)S(1)}, u32[]{:S(2)}, u32[]{:S(2)}) async-start(bf16[32,10,8,128]{3,2,1,0:T(8,128)(2,1)} %pad_maximum_fusion), calls=%async_computation | async-start | bytes 1310720 | tf_op jit(solution)/shard_map/all_to_all | solution.py:78
  20.9 0.0 copy-done
  20.9 0.3 fusion.9
  21.2 17.3 %all-to-all-done = bf16[32,10,8,128]{3,2,1,0:T(8,128)(2,1)S(1)} async-done(((bf16[32,10,8,128]{3,2,1,0:T(8,128)(2,1)}), bf16[32,10,8,128]{3,2,1,0:T(8,128)(2,1)S(1)}, u32[]{:S(2)}, u32[]{:S(2)}) %all-to-all-start) | async-done | bytes 655392 | tf_op jit(solution)/shard_map/all_to_all | solution.py:78
  38.5 0.1 convert_reduce_fusion
  38.5 0.9 %multiply_reduce_fusion = (f32[]{:T(128)}, f32[256,256]{1,0:T(8,128)S(1)}) fusion(bf16[256,1280]{1,0:T(8,128)(2,1)S(1)} %bitcast.58, f32[512]{0:T(512)S(1)} %dynamic-slice_bitcast_fusion), kind=kOutput, calls=%fused_computation.31 | convolution fusion | flops 67895296 | bytes 788484 | tf_op jit(solution)/shard_map/kp,jp->kj/dot_general | solution.py:31
  40.1 0.4 fusion.12
  40.6 0.4 fusion.7
  41.0 0.4 fusion.11
  41.4 0.4 fusion.46
  41.8 0.4 fusion.6
  42.2 0.4 fusion.48
  42.6 0.4 fusion.47
  43.0 0.4 fusion.5
  43.4 0.4 fusion.49
  43.7 0.4 fusion.50
  44.1 0.2 convolution_bitcast_fusion.1
  44.3 0.4 fusion.4
  44.7 0.4 convolution_divide_fusion
  45.1 0.3 convolution_bitcast_fusion
  45.4 0.3 fusion.51
  45.7 0.2 convert_reduce_fusion.1
  45.9 0.4 fusion.3
  46.3 19.5 %all_to_all.10 = bf16[32,6,8,128]{3,2,1,0:T(8,128)(2,1)S(1)} all-to-all(bf16[32,6,8,128]{3,2,1,0:T(8,128)(2,1)S(1)} %fusion.3), channel_id=1, replica_groups=mesh['member'=32,'region'=16] {'member'}, dimensions={0} | all-to-all | bytes 786432 | tf_op jit(solution)/shard_map/all_to_all | solution.py:92
  65.9 0.8 %copy.29 = bf16[8,32,6,128]{3,1,2,0:T(8,128)(2,1)} copy(bf16[8,32,6,128]{3,0,2,1:T(8,128)(2,1)S(1)} %bitcast.61) | data formatting | bytes 786432 | tf_op jit(solution)/shard_map/transpose | solution.py:93
  (6 shorter events, 0.1 us)
Async XLA Ops:
  0.0 20.9 %copy-start = (f32[32,4,128]{2,1,0:T(4,128)S(1)}, f32[32,4,128]{2,1,0:T(4,128)}, u32[]{:S(2)}) copy-start(f32[32,4,128]{2,1,0:T(4,128)} %param.9) | copy-start | bytes 196612
  0.8 3.9 %copy-start.3 = (s32[32,4]{0,1:T(4,128)S(1)}, s32[32,4]{0,1:T(4,128)}, u32[]{:S(2)}) copy-start(s32[32,4]{0,1:T(4,128)} %param.10) | copy-start | bytes 1540
  0.8 5.4 %collective-permute-start = (bf16[9,3,128]{2,1,0:T(4,128)(2,1)S(1)}, bf16[9,3,128]{2,1,0:T(4,128)(2,1)S(1)}, u32[]{:S(2)}, u32[]{:S(2)}) collective-permute-start(bf16[9,3,128]{2,1,0:T(4,128)(2,1)S(1)} %get-tuple-element.5), channel_id=1, source_target_pairs={{0,1},{1,2},{2,3},{3,4},{4,5},{5,6},{6,7},{7,8},{8,9},{9,10},{10,1... | collective-permute-start | bytes 20744 | tf_op jit(solution)/shard_map/ppermute | solution.py:16
  4.7 4.3 %collective-permute-start.1 = (bf16[9,3,128]{2,1,0:T(4,128)(2,1)S(1)}, bf16[9,3,128]{2,1,0:T(4,128)(2,1)S(1)}, u32[]{:S(2)}, u32[]{:S(2)}) collective-permute-start(bf16[9,3,128]{2,1,0:T(4,128)(2,1)S(1)} %get-tuple-element.6), channel_id=1, source_target_pairs={{1,0},{2,1},{3,2},{4,3},{5,4},{6,5},{7,6},{8,7},{9,8},{10,9},{11,1... | collective-permute-start | bytes 20744 | tf_op jit(solution)/shard_map/ppermute | solution.py:18
  4.9 4.1 %copy-start.1 = (bf16[8,32,128]{2,1,0:T(8,128)(2,1)S(1)}, bf16[8,32,128]{2,1,0:T(8,128)(2,1)}, u32[]{:S(2)}) copy-start(bf16[8,32,128]{2,1,0:T(8,128)(2,1)} %param.7) | copy-start | bytes 196612
  4.9 4.1 %copy-start.2 = (bf16[32,128]{1,0:T(8,128)(2,1)S(1)}, bf16[32,128]{1,0:T(8,128)(2,1)}, u32[]{:S(2)}) copy-start(bf16[32,128]{1,0:T(8,128)(2,1)} %param.8) | copy-start | bytes 24580
  10.5 27.9 %all-to-all-start = ((bf16[32,10,8,128]{3,2,1,0:T(8,128)(2,1)}), bf16[32,10,8,128]{3,2,1,0:T(8,128)(2,1)S(1)}, u32[]{:S(2)}, u32[]{:S(2)}) async-start(bf16[32,10,8,128]{3,2,1,0:T(8,128)(2,1)} %pad_maximum_fusion), calls=%async_computation | async-start | bytes 1310720 | tf_op jit(solution)/shard_map/all_to_all | solution.py:78

commit v2 on v1

v2 whole, which is shorter than its diff:
```python
import functools
import jax
import jax.numpy as jnp
from jax import lax
from jax.experimental import pallas as pl
from jax.experimental.pallas import tpu as pltpu
from jax.sharding import PartitionSpec as P

HW = 3
NS_STEPS = 5


def with_halo(cells, axis, dim, width):
    count = lax.axis_size(axis)
    head = lax.slice_in_dim(cells, 0, width, axis=dim)
    tail = lax.slice_in_dim(cells, cells.shape[dim] - width, cells.shape[dim], axis=dim)
    return jnp.concatenate(
        [
            lax.ppermute(tail, axis, [(i, (i + 1) % count) for i in range(count)]),
            cells,
            lax.ppermute(head, axis, [((i + 1) % count, i) for i in range(count)]),
        ],
        axis=dim,
    )


def halves(x):
    high = x.astype(jnp.bfloat16)
    return high, (x - high.astype(jnp.float32)).astype(jnp.bfloat16)


def dot(left, right, dims=((1,), (0,))):
    return lax.dot_general(left, right, (dims, ((), ())), preferred_element_type=jnp.float32)


def product(left, right):
    return dot(left[0], right[0]) + (dot(left[0], right[1]) + dot(left[1], right[0]))


def analyse_kernel(fields, live_ref, incoming_ref, loc_ref, innov_ref, out_ref):
    ranks, blocks, members, obs = incoming_ref.shape
    lines = ranks * members

    def rows(block):
        return incoming_ref[:, block].astype(jnp.float32).reshape(lines, obs)

    yb = jnp.concatenate([rows(block) for block in range(fields, blocks)], axis=1)
    scaled = (yb * loc_ref[...]).astype(jnp.bfloat16)
    left = jnp.concatenate([yb, jnp.broadcast_to(innov_ref[...], (16, yb.shape[1]))], axis=0)
    both = dot(left.astype(jnp.bfloat16), scaled, ((1,), (1,)))
    drive = both[lines : lines + 8]
    row = lax.broadcasted_iota(jnp.int32, (lines, lines), 0)
    column = lax.broadcasted_iota(jnp.int32, (lines, lines), 1)
    ident = (row == column).astype(jnp.float32)
    amat = ident + both[:lines] / jnp.float32(lines - 1)
    parts = halves(amat)
    square = product(parts, parts)
    total = jnp.sum(jnp.sum(amat * amat, axis=0, keepdims=True), axis=1, keepdims=True)
    frob = jnp.sqrt(total)
    inverse = 1.0 / frob
    joint = amat * inverse
    lower = 1.5 * ident - 0.5 * joint
    half = 1.5 * joint - (0.5 * inverse * inverse) * square
    joint = 1.5 * half - (0.5 * inverse) * product(halves(half), parts)
    for step in range(1, NS_STEPS):
        parts = halves(joint)
        if step + 1 < NS_STEPS:
            low = halves(lower)
            pair = tuple(jnp.concatenate([j, z], axis=0) for j, z in zip(parts, low))
            pair = product(pair, parts)
            half = 1.5 * joint - 0.5 * pair[:lines]
            lower = 1.5 * lower - 0.5 * pair[lines:]
            joint = 1.5 * half - 0.5 * product(halves(half), parts)
        else:
            lower = 1.5 * lower - 0.5 * product(halves(lower), parts)
    trans = lower * (1.0 / jnp.sqrt(frob))
    parts = halves(trans)
    inner = product(halves(drive), parts)
    wmean = product(halves(inner), parts) / jnp.float32(lines - 1)
    weights = (trans + wmean[:1]).astype(jnp.bfloat16)
    colsum = jnp.sum(weights.astype(jnp.float32), axis=1, keepdims=True)
    live = live_ref[0] > 0
    for pair in range(0, fields, 2):
        field = jnp.concatenate([rows(pair), rows(pair + 1)], axis=1)
        mean = jnp.sum(field, axis=0, keepdims=True) / jnp.float32(lines)
        mixed = dot(weights, field.astype(jnp.bfloat16)) + mean * (1.0 - colsum)
        mixed = jnp.where(live, mixed, field)
        for i in range(2):
            part = mixed[:, i * obs : (i + 1) * obs].reshape(ranks, members, obs)
            out_ref[:, pair + i] = part.astype(jnp.bfloat16)


def analyse(incoming, fields, loc, innov, live):
    ranks, blocks, members, obs = incoming.shape
    vmem = pl.BlockSpec(memory_space=pltpu.VMEM)
    return pl.pallas_call(
        functools.partial(analyse_kernel, fields),
        out_shape=jax.ShapeDtypeStruct((ranks, fields, members, obs), jnp.bfloat16),
        in_specs=[pl.BlockSpec(memory_space=pltpu.SMEM), vmem, vmem, vmem],
        out_specs=vmem,
        compiler_params=pltpu.CompilerParams(vmem_limit_bytes=32 * 2**20),
        name="analyse",
    )(live, incoming, loc, innov)


def one_hot_rows(indices, extent):
    return (indices.reshape(-1)[:, None] == jnp.arange(extent, dtype=jnp.int32)[None]).astype(
        jnp.bfloat16
    )


def shards(forecast, anomalies, misfit, precision, table, tally):
    members, slots, fields, cells = forecast.shape
    used = table.shape[1]
    obs = anomalies.shape[2]
    ranks = lax.axis_size("member")
    stacked = jnp.concatenate([anomalies, misfit[None]], axis=0)
    extended = with_halo(stacked, "region", 1, HW)
    extent = extended.shape[1]
    me = lax.axis_index("member")
    pick = one_hot_rows(table, extent)
    chosen = jnp.einsum(
        "qe,meo->qmo", pick, extended[:members], preferred_element_type=jnp.float32
    ).astype(jnp.bfloat16)
    chosen = chosen.reshape(slots, used, members, obs)
    outgoing = jnp.concatenate([jnp.transpose(forecast, (1, 2, 0, 3)), chosen], axis=1)
    incoming = lax.all_to_all(outgoing, "member", 0, 0, tiled=True)
    pick_mine = lax.dynamic_slice_in_dim(pick, me * used, used, 0)
    innov = jnp.dot(pick_mine, extended[members], preferred_element_type=jnp.float32).astype(
        jnp.bfloat16
    )
    innov = innov.reshape(1, used * obs).astype(jnp.float32)
    loc = lax.dynamic_slice_in_dim(precision, me, 1, 0).reshape(1, used * obs)
    live = (me < tally).astype(jnp.int32)
    back = analyse(incoming, fields, loc, innov, live)
    back = lax.all_to_all(back, "member", 0, 0, tiled=True)
    return jnp.transpose(back, (2, 0, 1, 3))


def solution(mesh):
    return jax.shard_map(
        shards,
        mesh=mesh,
        in_specs=(
            P("member", "region", None, None),
            P("member", "region", None),
            P("region", None),
            P("region", None, None),
            P("region", None),
            P("region"),
        ),
        out_specs=P("member", "region", None, None),
        check_vma=False,
    )
```

time: 67 us -> 63 us (0.940)
  matrix products: 7.3 us -> 0.54 us
  Pallas kernels: 0 us -> 4.04 us
  between operations: 1.59 us -> 0.75 us
    dot_general x17 -> x0, matrix products: 6.76 us -> none  [the longest x12 4.68 us: matmul_high(): return jnp.dot(left, right, precision=lax.Precision.HIGHEST)]
    pallas_call x0 -> x1, Pallas kernels: none -> 4.04 us  [analyse(): pl.pallas_call(functools.partial(analyse_kernel, fields), out_shape=jax.S...]
where the time goes in v2:
time: 63 us; the launch traced here: 62.8 us
  waiting for transfers between devices  20.1 us (32%)
  blocking collectives  19.5 us (31%)
  starting transfers between devices  13.5 us (21%)
  Pallas kernels  4.04 us (6%)
  local copies, waits for them, and re-layouts  2.53 us (4%)
  other arithmetic  1.76 us (3%)
  between operations  0.75 us (1%)
    all_to_all x1, blocking collectives, shards(): back = lax.all_to_all(back, 'member', 0, 0, tiled=True)  19.5 us
    all_to_all x1, waiting for transfers between devices, shards(): incoming = lax.all_to_all(outgoing, 'member', 0, 0, tiled=True)  17.3 us
    all_to_all x1, starting transfers between devices, shards(): incoming = lax.all_to_all(outgoing, 'member', 0, 0, tiled=True)  9.67 us
    pallas_call x1, Pallas kernels, analyse(): pl.pallas_call(functools.partial(analyse_kernel, fields), out_shape=jax.S...  4.04 us
    ppermute x1, starting transfers between devices, with_halo(): lax.ppermute(tail, axis, [(i, (i + 1) % count) for i in range(count)])  3.88 us
    ppermute x1, waiting for transfers between devices, with_halo(): lax.ppermute(head, axis, [((i + 1) % count, i) for i in range(count)])  2.78 us
    unnamed x10, local copies, waits for them, and re-layouts  1.4 us
  transfers between devices with their start and end apart: 3, of which 2 were waited for; matrix products, arithmetic and copies ran while one was open for 3% of the time, Pallas kernels for 0%

profile of v2, /device:TPU:193, one launch (start us, length us, event | category | flops | bytes accessed | tf_op | source)
XLA Modules:
  0.0 62.8 jit_solution(3797797233044257045)
XLA Ops:
  0.0 0.0 copy-start
  0.0 0.8 %pad_maximum_fusion.3 = (bf16[9,3,128]{2,1,0:T(4,128)(2,1)S(1)}, bf16[9,3,128]{2,1,0:T(4,128)(2,1)S(1)}) fusion(bf16[1,32,128]{2,1,0:T(8,128)(2,1)} %bitcast.20, bf16[8,32,128]{2,1,0:T(8,128)(2,1)} %param.7), kind=kLoop, calls=%fused_computation.18 | loop fusion | flops 27648 | bytes 87552 | tf_op jit(solution)/shard_map/slice | solution.py:16
  0.8 0.0 copy-start.3
  0.8 3.9 %collective-permute-start = (bf16[9,3,128]{2,1,0:T(4,128)(2,1)S(1)}, bf16[9,3,128]{2,1,0:T(4,128)(2,1)S(1)}, u32[]{:S(2)}, u32[]{:S(2)}) collective-permute-start(bf16[9,3,128]{2,1,0:T(4,128)(2,1)S(1)} %get-tuple-element.5), channel_id=1, source_target_pairs={{0,1},{1,2},{2,3},{3,4},{4,5},{5,6},{6,7},{7,8},{8,9},{9,10},{10,1... | collective-permute-start | bytes 20744 | tf_op jit(solution)/shard_map/ppermute | solution.py:19
  4.7 0.0 collective-permute-start.1
  4.7 0.0 copy-done.3
  4.7 0.1 copy.12
  4.8 0.1 eq.15
  4.9 0.0 copy-start.1
  4.9 0.0 copy-start.2
  4.9 1.3 %copy.16 = bf16[8,32,6,128]{3,0,2,1:T(8,128)(2,1)S(1)} copy(bf16[8,32,6,128]{3,1,2,0:T(8,128)(2,1)} %param.6) | data formatting | bytes 786432 | tf_op args[0]
  6.2 0.0 collective-permute-done
  6.2 2.8 %collective-permute-done.1 = bf16[9,3,128]{2,1,0:T(4,128)(2,1)S(1)} collective-permute-done((bf16[9,3,128]{2,1,0:T(4,128)(2,1)S(1)}, bf16[9,3,128]{2,1,0:T(4,128)(2,1)S(1)}, u32[]{:S(2)}, u32[]{:S(2)}) %collective-permute-start.1) | collective-permute-done | bytes 6944 | tf_op jit(solution)/shard_map/ppermute | solution.py:21
  9.0 0.0 copy-done.1
  9.0 0.0 copy-done.2
  9.0 0.3 convolution_convert_fusion
  9.3 0.2 copy.13
  9.5 0.9 %pad_maximum_fusion = bf16[32,10,8,128]{3,2,1,0:T(8,128)(2,1)} fusion(bf16[32,4,8,128]{3,2,1,0:T(8,128)(2,1)S(1)} %bitcast.19, bf16[32,6,8,128]{3,2,1,0:T(8,128)(2,1)S(1)} %bitcast.18), kind=kLoop, calls=%fused_computation.3 | loop fusion | flops 327680 | bytes 1310720 | tf_op jit(solution)/shard_map/concatenate | solution.py:126
  10.4 9.7 %all-to-all-start = ((bf16[32,10,8,128]{3,2,1,0:T(8,128)(2,1)}), bf16[32,10,8,128]{3,2,1,0:T(8,128)(2,1)S(1)}, u32[]{:S(2)}, u32[]{:S(2)}) async-start(bf16[32,10,8,128]{3,2,1,0:T(8,128)(2,1)} %pad_maximum_fusion), calls=%async_computation | async-start | bytes 1310720 | tf_op jit(solution)/shard_map/all_to_all | solution.py:127
  20.7 0.0 copy-done
  20.8 0.3 fusion
  21.0 17.3 %all-to-all-done.incoming_ref = bf16[32,10,8,128]{3,2,1,0:T(8,128)(2,1)S(1)} async-done(((bf16[32,10,8,128]{3,2,1,0:T(8,128)(2,1)}), bf16[32,10,8,128]{3,2,1,0:T(8,128)(2,1)S(1)}, u32[]{:S(2)}, u32[]{:S(2)}) %all-to-all-start) | async-done | bytes 655392 | tf_op jit(solution)/shard_map/all_to_all | solution.py:127
  38.3 4.0 %analyse.1 = bf16[32,6,8,128]{3,2,1,0:T(8,128)(2,1)S(1)} custom-call(s32[1]{0:T(128)S(6)} %convert_element_type.15.live_ref, bf16[32,10,8,128]{3,2,1,0:T(8,128)(2,1)S(1)} %all-to-all-done.incoming_ref, f32[1,512]{1,0:T(1,128)S(1)} %bitcast.16, f32[1,512]{1,0:T(1,128)S(1)} %bitcast.15), custom_call_target="tpu_custom_call" | custom-call | tf_op jit(solution)/shard_map/analyse/pallas_call | solution.py:96
  42.4 19.5 %all_to_all.10 = bf16[32,6,8,128]{3,2,1,0:T(8,128)(2,1)S(1)} all-to-all(bf16[32,6,8,128]{3,2,1,0:T(8,128)(2,1)S(1)} %analyse.1), channel_id=1, replica_groups=mesh['member'=32,'region'=16] {'member'}, dimensions={0} | all-to-all | bytes 786432 | tf_op jit(solution)/shard_map/all_to_all | solution.py:136
  61.9 0.8 %copy.14 = bf16[8,32,6,128]{3,1,2,0:T(8,128)(2,1)} copy(bf16[8,32,6,128]{3,0,2,1:T(8,128)(2,1)S(1)} %bitcast.17) | data formatting | bytes 786432 | tf_op jit(solution)/shard_map/transpose | solution.py:137
  (3 shorter events, 0.1 us)
Async XLA Ops:
  0.0 20.7 %copy-start = (f32[32,4,128]{2,1,0:T(4,128)S(1)}, f32[32,4,128]{2,1,0:T(4,128)}, u32[]{:S(2)}) copy-start(f32[32,4,128]{2,1,0:T(4,128)} %param.9) | copy-start | bytes 196612
  0.8 3.9 %copy-start.3 = (s32[32,4]{0,1:T(4,128)S(1)}, s32[32,4]{0,1:T(4,128)}, u32[]{:S(2)}) copy-start(s32[32,4]{0,1:T(4,128)} %param.10) | copy-start | bytes 1540
  0.8 5.4 %collective-permute-start = (bf16[9,3,128]{2,1,0:T(4,128)(2,1)S(1)}, bf16[9,3,128]{2,1,0:T(4,128)(2,1)S(1)}, u32[]{:S(2)}, u32[]{:S(2)}) collective-permute-start(bf16[9,3,128]{2,1,0:T(4,128)(2,1)S(1)} %get-tuple-element.5), channel_id=1, source_target_pairs={{0,1},{1,2},{2,3},{3,4},{4,5},{5,6},{6,7},{7,8},{8,9},{9,10},{10,1... | collective-permute-start | bytes 20744 | tf_op jit(solution)/shard_map/ppermute | solution.py:19
  4.7 4.3 %collective-permute-start.1 = (bf16[9,3,128]{2,1,0:T(4,128)(2,1)S(1)}, bf16[9,3,128]{2,1,0:T(4,128)(2,1)S(1)}, u32[]{:S(2)}, u32[]{:S(2)}) collective-permute-start(bf16[9,3,128]{2,1,0:T(4,128)(2,1)S(1)} %get-tuple-element.6), channel_id=1, source_target_pairs={{1,0},{2,1},{3,2},{4,3},{5,4},{6,5},{7,6},{8,7},{9,8},{10,9},{11,1... | collective-permute-start | bytes 20744 | tf_op jit(solution)/shard_map/ppermute | solution.py:21
  4.9 4.1 %copy-start.1 = (bf16[8,32,128]{2,1,0:T(8,128)(2,1)S(1)}, bf16[8,32,128]{2,1,0:T(8,128)(2,1)}, u32[]{:S(2)}) copy-start(bf16[8,32,128]{2,1,0:T(8,128)(2,1)} %param.7) | copy-start | bytes 196612
  4.9 4.1 %copy-start.2 = (bf16[32,128]{1,0:T(8,128)(2,1)S(1)}, bf16[32,128]{1,0:T(8,128)(2,1)}, u32[]{:S(2)}) copy-start(bf16[32,128]{1,0:T(8,128)(2,1)} %param.8) | copy-start | bytes 24580
  10.4 27.9 %all-to-all-start = ((bf16[32,10,8,128]{3,2,1,0:T(8,128)(2,1)}), bf16[32,10,8,128]{3,2,1,0:T(8,128)(2,1)S(1)}, u32[]{:S(2)}, u32[]{:S(2)}) async-start(bf16[32,10,8,128]{3,2,1,0:T(8,128)(2,1)} %pad_maximum_fusion), calls=%async_computation | async-start | bytes 1310720 | tf_op jit(solution)/shard_map/all_to_all | solution.py:127

commit v3 on v2

v3 whole, which is shorter than its diff:
```python
import functools
import jax
import jax.numpy as jnp
from jax import lax
from jax.experimental import pallas as pl
from jax.experimental.pallas import tpu as pltpu
from jax.sharding import PartitionSpec as P

HW = 3
NS_STEPS = 5
VMEM = pl.BlockSpec(memory_space=pltpu.VMEM)
SMEM = pl.BlockSpec(memory_space=pltpu.SMEM)
PARAMS = pltpu.CompilerParams(vmem_limit_bytes=32 * 2**20)


def split(x):
    high = x.astype(jnp.bfloat16)
    return high, (x - high.astype(jnp.float32)).astype(jnp.bfloat16)


def halves(x):
    return jnp.concatenate(split(x), axis=0)


def dot(left, right, dims=((1,), (0,))):
    return lax.dot_general(left, right, (dims, ((), ())), preferred_element_type=jnp.float32)


def narrow(left, right):
    return dot(left.astype(jnp.bfloat16), right.astype(jnp.bfloat16))


def analyse_kernel(
    fields, me_ref, tally_ref, table_ref, incoming_ref, loc_ref, misfit_ref, before_ref, after_ref, out_ref, line_ref
):
    ranks, blocks, members, obs = incoming_ref.shape
    lines = ranks * members
    count = misfit_ref.shape[0]
    me = me_ref[0]

    def rows(block):
        return incoming_ref[:, block].astype(jnp.float32).reshape(lines, obs)

    def across(x):
        return jnp.sum(jnp.sum(x, axis=0, keepdims=True), axis=1, keepdims=True)

    line_ref[HW : HW + count] = misfit_ref[...].astype(jnp.float32)
    for i in range(HW):
        line_ref[i : i + 1] = before_ref[members, i : i + 1].astype(jnp.float32)
        line_ref[HW + count + i : HW + count + i + 1] = after_ref[members, i : i + 1].astype(jnp.float32)
    innov = jnp.concatenate([line_ref[pl.ds(table_ref[h, me], 1)] for h in range(blocks - fields)], axis=1)
    loc = loc_ref[me]
    loc = jnp.concatenate([loc[h : h + 1] for h in range(blocks - fields)], axis=1)
    yb = jnp.concatenate([rows(block) for block in range(fields, blocks)], axis=1)
    scaled = (yb * loc).astype(jnp.bfloat16)
    left = jnp.concatenate([yb, jnp.broadcast_to(innov, (16, yb.shape[1]))], axis=0)
    both = dot(left.astype(jnp.bfloat16), scaled, ((1,), (1,)))
    drive = both[lines : lines + 8]
    row = lax.broadcasted_iota(jnp.int32, (lines, lines), 0)
    column = lax.broadcasted_iota(jnp.int32, (lines, lines), 1)
    ident = (row == column).astype(jnp.float32)
    gram = both[:lines] * (1.0 / (lines - 1))
    amat = gram + ident
    thin, low = split(gram)
    pair = halves(drive)
    square = dot(jnp.concatenate([thin, pair], axis=0), thin)
    tail = square[lines:] + dot(pair, low)
    inverse = lax.rsqrt(across(amat * amat))
    root = jnp.sqrt(inverse)
    centre = across(amat * ident) * (1.0 / lines)

    w, n = inverse, gram * inverse
    t = 1.5 * w - 0.5 * w * w
    h = (1.5 - w) * n - (0.5 * inverse * inverse) * square[:lines]
    vector = (1.5 - 0.5 * w) * drive - (0.5 * inverse) * (tail[:8] + tail[8:])
    n = (1.5 - 0.5 * w) * h - (0.5 * t) * n - 0.5 * narrow(h, n)
    w = 1.5 * t - 0.5 * t * w
    mean = centre * inverse
    z = 1.5 - 0.5 * mean
    r = (-0.5 * inverse) * (gram - (centre - 1.0) * ident)
    mean = mean * z * z
    n = n - (mean - w) * ident
    w = mean
    for step in range(1, NS_STEPS):
        thin, low = split(n)
        last = step + 1 == NS_STEPS
        left = [r.astype(jnp.bfloat16), halves(vector)]
        both = dot(jnp.concatenate(left if last else [thin] + left, axis=0), thin)
        slope = 1.5 - 0.5 * w
        tail = both[both.shape[0] - 16 :] + dot(left[1], low)
        vector = slope * vector - 0.5 * (tail[:8] + tail[8:])
        r = slope * r - (0.5 * z) * n - 0.5 * both[both.shape[0] - 16 - lines : both.shape[0] - 16]
        z = z * slope
        if not last:
            t = slope * w
            h = (1.5 - w) * n - 0.5 * both[:lines]
            n = slope * h - (0.5 * t) * n - 0.5 * dot(h.astype(jnp.bfloat16), thin)
            w = slope * t
    high, low = split(r)
    tail = dot(halves(vector), high) + dot(halves(vector), low)
    wmean = (z * vector + (tail[:8] + tail[8:])) * (root * root * (1.0 / (lines - 1)))
    trans = (r + z * ident) * root
    weights = (trans + wmean[:1]).astype(jnp.bfloat16)
    colsum = jnp.sum(weights.astype(jnp.float32), axis=1, keepdims=True)
    live = me < tally_ref[0]
    for pair in range(0, fields, 2):
        field = jnp.concatenate([rows(pair), rows(pair + 1)], axis=1)
        mean = jnp.sum(field, axis=0, keepdims=True) * (1.0 / lines)
        mixed = dot(weights, field.astype(jnp.bfloat16)) + mean * (1.0 - colsum)
        mixed = jnp.where(live, mixed, field)
        for i in range(2):
            part = mixed[:, i * obs : (i + 1) * obs].reshape(ranks, members, obs)
            out_ref[:, pair + i] = part.astype(jnp.bfloat16)


def pack_kernel(table_ref, forecast_ref, anomalies_ref, out_ref, blocks_ref, held_ref, sems):
    fields = forecast_ref.shape[1]
    copies = [
        pltpu.make_async_copy(forecast_ref.at[:, field], held_ref.at[field], sems.at[field])
        for field in range(fields)
    ]
    for copy in copies:
        copy.start()
    blocks_ref[...] = jnp.swapaxes(anomalies_ref[...], 0, 1)
    for field in range(fields):
        copies[field].wait()
        out_ref[:, field] = jnp.swapaxes(held_ref[field], 0, 1)


def choose_kernel(fields, table_ref, packed_ref, blocks_ref, before_ref, after_ref, out_ref, all_ref):
    count, members, _ = blocks_ref.shape
    all_ref[HW : HW + count] = blocks_ref[...]
    all_ref[:HW] = jnp.swapaxes(before_ref[:members], 0, 1)
    all_ref[HW + count :] = jnp.swapaxes(after_ref[:members], 0, 1)
    out_ref[:, :fields] = packed_ref[...]
    used, slots = table_ref.shape
    for slot in range(slots):
        for h in range(used):
            out_ref[slot, fields + h] = all_ref[table_ref[h, slot]]


def shards(forecast, anomalies, misfit, precision, table, tally):
    members, slots, fields, cells = forecast.shape
    used = table.shape[1]
    count, obs = misfit.shape
    table = jnp.transpose(table)
    ranks = lax.axis_size("member")
    regions = lax.axis_size("region")
    stacked = jnp.concatenate([anomalies, misfit[None]], axis=0)
    up = [(i, (i + 1) % regions) for i in range(regions)]
    before = lax.ppermute(stacked[:, count - HW :], "region", up)
    after = lax.ppermute(stacked[:, :HW], "region", [(j, i) for i, j in up])
    packed, blocks = pl.pallas_call(
        pack_kernel,
        out_shape=(
            jax.ShapeDtypeStruct((slots, fields, members, cells), forecast.dtype),
            jax.ShapeDtypeStruct((count, members, obs), anomalies.dtype),
        ),
        in_specs=[VMEM, pl.BlockSpec(memory_space=pl.ANY), VMEM],
        out_specs=(VMEM, VMEM),
        scratch_shapes=[
            pltpu.VMEM((fields, members, slots, cells), forecast.dtype),
            pltpu.SemaphoreType.DMA((fields,)),
        ],
        compiler_params=PARAMS,
        name="pack",
    )(table, jnp.transpose(forecast, (0, 2, 1, 3)), anomalies)
    outgoing = pl.pallas_call(
        functools.partial(choose_kernel, fields),
        out_shape=jax.ShapeDtypeStruct((slots, fields + used, members, cells), packed.dtype),
        in_specs=[SMEM, VMEM, VMEM, VMEM, VMEM],
        out_specs=VMEM,
        scratch_shapes=[pltpu.VMEM((count + 2 * HW, members, obs), blocks.dtype)],
        compiler_params=PARAMS,
        name="choose",
    )(table, packed, blocks, before, after)
    incoming = lax.all_to_all(outgoing, "member", 0, 0, tiled=True)
    me = lax.axis_index("member").reshape(1)
    back = pl.pallas_call(
        functools.partial(analyse_kernel, fields),
        out_shape=jax.ShapeDtypeStruct((ranks, fields, members, cells), forecast.dtype),
        in_specs=[SMEM, SMEM, SMEM, VMEM, VMEM, VMEM, VMEM, VMEM],
        out_specs=VMEM,
        scratch_shapes=[pltpu.VMEM((count + 2 * HW, obs), jnp.float32)],
        compiler_params=PARAMS,
        name="analyse",
    )(me, tally, table, incoming, precision, misfit, before, after)
    back = lax.all_to_all(back, "member", 0, 0, tiled=True)
    return jnp.transpose(back, (2, 0, 1, 3))


def solution(mesh):
    return jax.shard_map(
        shards,
        mesh=mesh,
        in_specs=(
            P("member", "region", None, None),
            P("member", "region", None),
            P("region", None),
            P("region", None, None),
            P("region", None),
            P("region"),
        ),
        out_specs=P("member", "region", None, None),
        check_vma=False,
    )
```

time: 63 us -> 62.2 us (0.987)
  other arithmetic: 1.76 us -> 0.81 us
    slice x1 -> x0, other arithmetic: 0.81 us -> none  [with_halo(): lax.slice_in_dim(cells, cells.shape[dim] - width, cells.shape[dim], axis=...]
    pallas_call x1 -> x3, Pallas kernels: 4.04 us -> 4.64 us  [the longest x1 2.82 us: shards(): pl.pallas_call(functools.partial(analyse_kernel, fields), out_shape=jax.S...]
  transfers between devices with their start and end apart: 3 -> 3, of which waited for: 2 -> 2; matrix products, arithmetic and copies ran while one was open for 3% -> 0% of each run, Pallas kernels for 0% -> 0%
where the time goes in v3:
time: 62.2 us; the launch traced here: 61.8 us
  waiting for transfers between devices  19.9 us (32%)
  blocking collectives  19.5 us (31%)
  starting transfers between devices  13.7 us (22%)
  Pallas kernels  4.64 us (7%)
  local copies, waits for them, and re-layouts  2.53 us (4%)
  other arithmetic  0.81 us (1%)
  between operations  0.71 us (1%)
    all_to_all x1, blocking collectives, shards(): back = lax.all_to_all(back, 'member', 0, 0, tiled=True)  19.5 us
    all_to_all x1, waiting for transfers between devices, shards(): incoming = lax.all_to_all(outgoing, 'member', 0, 0, tiled=True)  17.6 us
    all_to_all x1, starting transfers between devices, shards(): incoming = lax.all_to_all(outgoing, 'member', 0, 0, tiled=True)  9.8 us
    ppermute x1, starting transfers between devices, shards(): before = lax.ppermute(stacked[:, count - HW:], 'region', up)  3.88 us
    pallas_call x1, Pallas kernels, shards(): pl.pallas_call(functools.partial(analyse_kernel, fields), out_shape=jax.S...  2.82 us
    ppermute x1, waiting for transfers between devices, shards(): after = lax.ppermute(stacked[:, :HW], 'region', [(j, i) for i, j in up])  2.32 us
    unnamed x10, local copies, waits for them, and re-layouts  1.68 us
    pallas_call x1, Pallas kernels, shards(): pl.pallas_call(functools.partial(choose_kernel, fields), out_shape=jax.Sh...  1.54 us
  transfers between devices with their start and end apart: 3, of which 2 were waited for; matrix products, arithmetic and copies ran while one was open for 0% of the time, Pallas kernels for 0%

profile of v3, /device:TPU:193, one launch (start us, length us, event | category | flops | bytes accessed | tf_op | source)
XLA Modules:
  0.0 61.8 jit_solution(13451921110719774074)
XLA Ops:
  0.0 0.0 copy-start.1
  0.0 0.8 %pad_maximum_fusion = (bf16[9,3,128]{2,1,0:T(4,128)(2,1)S(1)}, bf16[9,3,128]{2,1,0:T(4,128)(2,1)S(1)}) fusion(bf16[1,32,128]{2,1,0:T(8,128)(2,1)} %bitcast.6, bf16[8,32,128]{2,1,0:T(8,128)(2,1)} %anomalies_ref.1), kind=kLoop, calls=%fused_computation | loop fusion | flops 27648 | bytes 87552 | tf_op jit(solution)/shard_map/concatenate | solution.py:149
  0.8 3.9 %collective-permute-start = (bf16[9,3,128]{2,1,0:T(4,128)(2,1)S(1)}, bf16[9,3,128]{2,1,0:T(4,128)(2,1)S(1)}, u32[]{:S(2)}, u32[]{:S(2)}) collective-permute-start(bf16[9,3,128]{2,1,0:T(4,128)(2,1)S(1)} %get-tuple-element.10), channel_id=1, source_target_pairs={{0,1},{1,2},{2,3},{3,4},{4,5},{5,6},{6,7},{7,8},{8,9},{9,10},{10,1... | collective-permute-start | bytes 20744 | tf_op jit(solution)/shard_map/ppermute | solution.py:151
  4.7 0.0 copy-start.4
  4.7 0.0 collective-permute-start.1
  4.7 0.0 copy-done.1
  4.7 0.7 %copy-done.4 = s32[32,4]{0,1:T(4,128)S(1)} copy-done((s32[32,4]{0,1:T(4,128)S(1)}, s32[32,4]{0,1:T(4,128)}, u32[]{:S(2)}) %copy-start.4) | copy-done | bytes 536
  5.4 0.0 copy-start
  5.4 1.0 %copy-done = bf16[8,32,6,128]{3,1,2,0:T(8,128)(2,1)S(1)} copy-done((bf16[8,32,6,128]{3,1,2,0:T(8,128)(2,1)S(1)}, bf16[8,32,6,128]{3,1,2,0:T(8,128)(2,1)}, u32[]{:S(2)}) %copy-start) | copy-done | bytes 393240
  6.4 0.3 pack.1
  6.7 0.0 collective-permute-done.before_ref
  6.7 2.3 %collective-permute-done.1.after_ref = bf16[9,3,128]{2,1,0:T(4,128)(2,1)S(1)} collective-permute-done((bf16[9,3,128]{2,1,0:T(4,128)(2,1)S(1)}, bf16[9,3,128]{2,1,0:T(4,128)(2,1)S(1)}, u32[]{:S(2)}, u32[]{:S(2)}) %collective-permute-start.1) | collective-permute-done | bytes 6944 | tf_op jit(solution)/shard_map/ppermute | solution.py:152
  9.0 1.5 %choose.1 = bf16[32,10,8,128]{3,2,1,0:T(8,128)(2,1)} custom-call(s32[4,32]{1,0:T(4,128)S(1)} %bitcast.8, bf16[32,6,8,128]{3,2,1,0:T(8,128)(2,1)S(1)} %get-tuple-element.7.packed_ref, bf16[32,8,128]{2,1,0:T(8,128)(2,1)S(1)} %get-tuple-element.8.blocks_ref, bf16[9,3,128]{2,1,0:T(4,128)(2,1)S(1)} %collective-permute-done.before_ref, ...), custom_call_target="tpu_custom_call" | custom-call | tf_op jit(solution)/shard_map/choose/pallas_call | solution.py:168
  10.5 0.0 copy-start.2
  10.5 9.8 %all-to-all-start = ((bf16[32,10,8,128]{3,2,1,0:T(8,128)(2,1)}), bf16[32,10,8,128]{3,2,1,0:T(8,128)(2,1)S(1)}, u32[]{:S(2)}, u32[]{:S(2)}) async-start(bf16[32,10,8,128]{3,2,1,0:T(8,128)(2,1)} %choose.1), calls=%async_computation | async-start | bytes 1310720 | tf_op jit(solution)/shard_map/all_to_all | solution.py:177
  20.3 0.0 copy-start.3
  21.0 17.6 %all-to-all-done.incoming_ref = bf16[32,10,8,128]{3,2,1,0:T(8,128)(2,1)S(1)} async-done(((bf16[32,10,8,128]{3,2,1,0:T(8,128)(2,1)}), bf16[32,10,8,128]{3,2,1,0:T(8,128)(2,1)S(1)}, u32[]{:S(2)}, u32[]{:S(2)}) %all-to-all-start) | async-done | bytes 655392 | tf_op jit(solution)/shard_map/all_to_all | solution.py:177
  38.6 0.0 copy-done.2
  38.6 0.0 copy-done.3
  38.6 2.8 %analyse.1 = bf16[32,6,8,128]{3,2,1,0:T(8,128)(2,1)S(1)} custom-call(s32[1]{0:T(128)} %bitcast.me_ref, s32[1]{0:T(128)S(6)} %copy.8.tally_ref, s32[4,32]{1,0:T(4,128)S(1)} %bitcast.9, bf16[32,10,8,128]{3,2,1,0:T(8,128)(2,1)S(1)} %all-to-all-done.incoming_ref, f32[32,4,128]{2,1,0:T(4,128)S(1)} %copy-done.2, bf16[32,128]{1,0:T(8,128)(2,1)S(1)} %copy-done.3, ...), custom_call_target="tpu_custom_call" | custom-call | tf_op jit(solution)/shard_map/analyse/pallas_call | solution.py:179
  41.4 19.5 %all_to_all.10 = bf16[32,6,8,128]{3,2,1,0:T(8,128)(2,1)S(1)} all-to-all(bf16[32,6,8,128]{3,2,1,0:T(8,128)(2,1)S(1)} %analyse.1), channel_id=1, replica_groups=mesh['member'=32,'region'=16] {'member'}, dimensions={0} | all-to-all | bytes 786432 | tf_op jit(solution)/shard_map/all_to_all | solution.py:188
  61.0 0.8 %copy.7 = bf16[8,32,6,128]{3,1,2,0:T(8,128)(2,1)} copy(bf16[8,32,6,128]{3,0,2,1:T(8,128)(2,1)S(1)} %bitcast.10) | data formatting | bytes 786432 | tf_op jit(solution)/shard_map/transpose | solution.py:189
Async XLA Ops:
  0.0 4.7 %copy-start.1 = (bf16[8,32,128]{2,1,0:T(8,128)(2,1)S(1)}, bf16[8,32,128]{2,1,0:T(8,128)(2,1)}, u32[]{:S(2)}) copy-start(bf16[8,32,128]{2,1,0:T(8,128)(2,1)} %anomalies_ref.1) | copy-start | bytes 196612
  0.8 5.8 %collective-permute-start = (bf16[9,3,128]{2,1,0:T(4,128)(2,1)S(1)}, bf16[9,3,128]{2,1,0:T(4,128)(2,1)S(1)}, u32[]{:S(2)}, u32[]{:S(2)}) collective-permute-start(bf16[9,3,128]{2,1,0:T(4,128)(2,1)S(1)} %get-tuple-element.10), channel_id=1, source_target_pairs={{0,1},{1,2},{2,3},{3,4},{4,5},{5,6},{6,7},{7,8},{8,9},{9,10},{10,1... | collective-permute-start | bytes 20744 | tf_op jit(solution)/shard_map/ppermute | solution.py:151
  4.7 0.7 %copy-start.4 = (s32[32,4]{0,1:T(4,128)S(1)}, s32[32,4]{0,1:T(4,128)}, u32[]{:S(2)}) copy-start(s32[32,4]{0,1:T(4,128)} %param.10) | copy-start | bytes 1540
  4.7 4.3 %collective-permute-start.1 = (bf16[9,3,128]{2,1,0:T(4,128)(2,1)S(1)}, bf16[9,3,128]{2,1,0:T(4,128)(2,1)S(1)}, u32[]{:S(2)}, u32[]{:S(2)}) collective-permute-start(bf16[9,3,128]{2,1,0:T(4,128)(2,1)S(1)} %get-tuple-element.9), channel_id=1, source_target_pairs={{1,0},{2,1},{3,2},{4,3},{5,4},{6,5},{7,6},{8,7},{9,8},{10,9},{11,1... | collective-permute-start | bytes 20744 | tf_op jit(solution)/shard_map/ppermute | solution.py:152
  5.4 1.0 %copy-start = (bf16[8,32,6,128]{3,1,2,0:T(8,128)(2,1)S(1)}, bf16[8,32,6,128]{3,1,2,0:T(8,128)(2,1)}, u32[]{:S(2)}) copy-start(bf16[8,32,6,128]{3,1,2,0:T(8,128)(2,1)} %param.6) | copy-start | bytes 1179652
  10.5 28.0 %copy-start.2 = (f32[32,4,128]{2,1,0:T(4,128)S(1)}, f32[32,4,128]{2,1,0:T(4,128)}, u32[]{:S(2)}) copy-start(f32[32,4,128]{2,1,0:T(4,128)} %loc_ref.1) | copy-start | bytes 196612
  10.5 28.0 %all-to-all-start = ((bf16[32,10,8,128]{3,2,1,0:T(8,128)(2,1)}), bf16[32,10,8,128]{3,2,1,0:T(8,128)(2,1)S(1)}, u32[]{:S(2)}, u32[]{:S(2)}) async-start(bf16[32,10,8,128]{3,2,1,0:T(8,128)(2,1)} %choose.1), calls=%async_computation | async-start | bytes 1310720 | tf_op jit(solution)/shard_map/all_to_all | solution.py:177
  20.3 18.2 %copy-start.3 = (bf16[32,128]{1,0:T(8,128)(2,1)S(1)}, bf16[32,128]{1,0:T(8,128)(2,1)}, u32[]{:S(2)}) copy-start(bf16[32,128]{1,0:T(8,128)(2,1)} %misfit_ref.1) | copy-start | bytes 24580

commit v4 on v3

--- a/solution.py
+++ b/solution.py
@@ -30,13 +30,9 @@
     return dot(left.astype(jnp.bfloat16), right.astype(jnp.bfloat16))
 
 
-def analyse_kernel(
-    fields, me_ref, tally_ref, table_ref, incoming_ref, loc_ref, misfit_ref, before_ref, after_ref, out_ref, line_ref
-):
+def analyse_kernel(fields, incoming_ref, side_ref, out_ref):
     ranks, blocks, members, obs = incoming_ref.shape
     lines = ranks * members
-    count = misfit_ref.shape[0]
-    me = me_ref[0]
 
     def rows(block):
         return incoming_ref[:, block].astype(jnp.float32).reshape(lines, obs)
@@ -44,13 +40,7 @@
     def across(x):
         return jnp.sum(jnp.sum(x, axis=0, keepdims=True), axis=1, keepdims=True)
 
-    line_ref[HW : HW + count] = misfit_ref[...].astype(jnp.float32)
-    for i in range(HW):
-        line_ref[i : i + 1] = before_ref[members, i : i + 1].astype(jnp.float32)
-        line_ref[HW + count + i : HW + count + i + 1] = after_ref[members, i : i + 1].astype(jnp.float32)
-    innov = jnp.concatenate([line_ref[pl.ds(table_ref[h, me], 1)] for h in range(blocks - fields)], axis=1)
-    loc = loc_ref[me]
-    loc = jnp.concatenate([loc[h : h + 1] for h in range(blocks - fields)], axis=1)
+    loc, innov, live = side_ref[0:1], side_ref[1:2], side_ref[2:3, : 2 * obs] > 0
     yb = jnp.concatenate([rows(block) for block in range(fields, blocks)], axis=1)
     scaled = (yb * loc).astype(jnp.bfloat16)
     left = jnp.concatenate([yb, jnp.broadcast_to(innov, (16, yb.shape[1]))], axis=0)
@@ -102,7 +92,6 @@
     trans = (r + z * ident) * root
     weights = (trans + wmean[:1]).astype(jnp.bfloat16)
     colsum = jnp.sum(weights.astype(jnp.float32), axis=1, keepdims=True)
-    live = me < tally_ref[0]
     for pair in range(0, fields, 2):
         field = jnp.concatenate([rows(pair), rows(pair + 1)], axis=1)
         mean = jnp.sum(field, axis=0, keepdims=True) * (1.0 / lines)
@@ -113,22 +102,22 @@
             out_ref[:, pair + i] = part.astype(jnp.bfloat16)
 
 
-def pack_kernel(table_ref, forecast_ref, anomalies_ref, out_ref, blocks_ref, held_ref, sems):
-    fields = forecast_ref.shape[1]
-    copies = [
-        pltpu.make_async_copy(forecast_ref.at[:, field], held_ref.at[field], sems.at[field])
-        for field in range(fields)
-    ]
-    for copy in copies:
-        copy.start()
+def edges_kernel(tail_ref, head_ref, tail_out_ref, head_out_ref):
+    tail_out_ref[...] = tail_ref[...]
+    head_out_ref[...] = head_ref[...]
+
+
+def pack_kernel(table_ref, loc_ref, misfit_ref, forecast_ref, anomalies_ref, out_ref, blocks_ref):
+    for field in range(forecast_ref.shape[1]):
+        out_ref[:, field] = jnp.swapaxes(forecast_ref[:, field], 0, 1)
     blocks_ref[...] = jnp.swapaxes(anomalies_ref[...], 0, 1)
-    for field in range(fields):
-        copies[field].wait()
-        out_ref[:, field] = jnp.swapaxes(held_ref[field], 0, 1)
-
-
-def choose_kernel(fields, table_ref, packed_ref, blocks_ref, before_ref, after_ref, out_ref, all_ref):
-    count, members, _ = blocks_ref.shape
+
+
+def choose_kernel(
+    fields, place_ref, table_ref, packed_ref, blocks_ref, loc_ref, misfit_ref, before_ref, after_ref,
+    out_ref, side_ref, all_ref, line_ref
+):
+    count, members, obs = blocks_ref.shape
     all_ref[HW : HW + count] = blocks_ref[...]
     all_ref[:HW] = jnp.swapaxes(before_ref[:members], 0, 1)
     all_ref[HW + count :] = jnp.swapaxes(after_ref[:members], 0, 1)
@@ -137,6 +126,17 @@
     for slot in range(slots):
         for h in range(used):
             out_ref[slot, fields + h] = all_ref[table_ref[h, slot]]
+    dead = place_ref[0] >= slots
+    me = jnp.where(dead, place_ref[0] - slots, place_ref[0])
+    line_ref[HW : HW + count] = misfit_ref[...].astype(jnp.float32)
+    line_ref[:HW] = before_ref[members].astype(jnp.float32)
+    line_ref[HW + count :] = after_ref[members].astype(jnp.float32)
+    loc = loc_ref[me]
+    side_ref[...] = jnp.full(side_ref.shape, jnp.where(dead, 0.0, 1.0), jnp.float32)
+    for h in range(used):
+        at = slice(h * obs, (h + 1) * obs)
+        side_ref[0:1, at] = loc[h : h + 1]
+        side_ref[1:2, at] = line_ref[pl.ds(table_ref[h, me], 1)]
 
 
 def shards(forecast, anomalies, misfit, precision, table, tally):
@@ -148,43 +148,55 @@
     regions = lax.axis_size("region")
     stacked = jnp.concatenate([anomalies, misfit[None]], axis=0)
     up = [(i, (i + 1) % regions) for i in range(regions)]
-    before = lax.ppermute(stacked[:, count - HW :], "region", up)
-    after = lax.ppermute(stacked[:, :HW], "region", [(j, i) for i, j in up])
+    edge = jax.ShapeDtypeStruct((members + 1, HW, obs), anomalies.dtype)
+    tail, head = pl.pallas_call(
+        edges_kernel,
+        out_shape=(edge, edge),
+        in_specs=[VMEM, VMEM],
+        out_specs=(VMEM, VMEM),
+        compiler_params=PARAMS,
+        cost_estimate=pl.CostEstimate(flops=8 * 10**9, bytes_accessed=10**6, transcendentals=0),
+        name="edges",
+    )(stacked[:, count - HW :], stacked[:, :HW])
+    before = lax.ppermute(tail, "region", up)
+    after = lax.ppermute(head, "region", [(j, i) for i, j in up])
     packed, blocks = pl.pallas_call(
         pack_kernel,
         out_shape=(
             jax.ShapeDtypeStruct((slots, fields, members, cells), forecast.dtype),
             jax.ShapeDtypeStruct((count, members, obs), anomalies.dtype),
         ),
-        in_specs=[VMEM, pl.BlockSpec(memory_space=pl.ANY), VMEM],
+        in_specs=[VMEM] * 5,
+        out_specs=(VMEM, VMEM),
+        compiler_params=PARAMS,
+        name="pack",
+    )(table, precision, misfit, jnp.transpose(forecast, (0, 2, 1, 3)), anomalies)
+    me = lax.axis_index("member").reshape(1)
+    place = me + slots * (me >= tally).astype(jnp.int32)
+    outgoing, side = pl.pallas_call(
+        functools.partial(choose_kernel, fields),
+        out_shape=(
+            jax.ShapeDtypeStruct((slots, fields + used, members, cells), packed.dtype),
+            jax.ShapeDtypeStruct((8, used * obs), jnp.float32),
+        ),
+        in_specs=[SMEM, SMEM] + [VMEM] * 6,
         out_specs=(VMEM, VMEM),
         scratch_shapes=[
-            pltpu.VMEM((fields, members, slots, cells), forecast.dtype),
-            pltpu.SemaphoreType.DMA((fields,)),
+            pltpu.VMEM((count + 2 * HW, members, obs), blocks.dtype),
+            pltpu.VMEM((count + 2 * HW, obs), jnp.float32),
         ],
         compiler_params=PARAMS,
-        name="pack",
-    )(table, jnp.transpose(forecast, (0, 2, 1, 3)), anomalies)
-    outgoing = pl.pallas_call(
-        functools.partial(choose_kernel, fields),
-        out_shape=jax.ShapeDtypeStruct((slots, fields + used, members, cells), packed.dtype),
-        in_specs=[SMEM, VMEM, VMEM, VMEM, VMEM],
-        out_specs=VMEM,
-        scratch_shapes=[pltpu.VMEM((count + 2 * HW, members, obs), blocks.dtype)],
-        compiler_params=PARAMS,
         name="choose",
-    )(table, packed, blocks, before, after)
+    )(place, table, packed, blocks, precision, misfit, before, after)
     incoming = lax.all_to_all(outgoing, "member", 0, 0, tiled=True)
-    me = lax.axis_index("member").reshape(1)
     back = pl.pallas_call(
         functools.partial(analyse_kernel, fields),
         out_shape=jax.ShapeDtypeStruct((ranks, fields, members, cells), forecast.dtype),
-        in_specs=[SMEM, SMEM, SMEM, VMEM, VMEM, VMEM, VMEM, VMEM],
+        in_specs=[VMEM, VMEM],
         out_specs=VMEM,
-        scratch_shapes=[pltpu.VMEM((count + 2 * HW, obs), jnp.float32)],
         compiler_params=PARAMS,
         name="analyse",
-    )(me, tally, table, incoming, precision, misfit, before, after)
+    )(incoming, side)
     back = lax.all_to_all(back, "member", 0, 0, tiled=True)
     return jnp.transpose(back, (2, 0, 1, 3))
 

time: 62.2 us -> 60.4 us (0.971)
  blocking collectives: 19.5 us -> 47.2 us
  waiting for transfers between devices: 19.9 us -> 2.8 us
  starting transfers between devices: 13.7 us -> 3.88 us
  Pallas kernels: 4.64 us -> 3.1 us
  local copies, waits for them, and re-layouts: 2.53 us -> 1.51 us
    all_to_all x0 -> x1, blocking collectives: none -> 27.7 us  [shards(): incoming = lax.all_to_all(outgoing, 'member', 0, 0, tiled=True)]
    all_to_all x1 -> x0, waiting for transfers between devices: 17.6 us -> none  [shards(): incoming = lax.all_to_all(outgoing, 'member', 0, 0, tiled=True)]
    all_to_all x1 -> x0, starting transfers between devices: 9.8 us -> none  [shards(): incoming = lax.all_to_all(outgoing, 'member', 0, 0, tiled=True)]
    unnamed x10, local copies, waits for them, and re-layouts: 1.68 us -> 0.66 us
    pallas_call x1 -> x2, Pallas kernels: 1.54 us -> 0.72 us  [the longest x1 0.71 us: shards(): pl.pallas_call(functools.partial(choose_kernel, fields), out_shape=(jax.S...]
  transfers between devices with their start and end apart: 3 -> 2, of which waited for: 2 -> 1; matrix products, arithmetic and copies ran while one was open for 0% -> 0% of each run, Pallas kernels for 0% -> 0%
where the time goes in v4:
time: 60.4 us; the launch traced here: 60.1 us
  blocking collectives  47.2 us (78%)
  starting transfers between devices  3.88 us (6%)
  Pallas kernels  3.1 us (5%)
  waiting for transfers between devices  2.8 us (5%)
  local copies, waits for them, and re-layouts  1.51 us (2%)
  other arithmetic  0.78 us (1%)
  between operations  0.78 us (1%)
    all_to_all x1, blocking collectives, shards(): incoming = lax.all_to_all(outgoing, 'member', 0, 0, tiled=True)  27.7 us
    all_to_all x1, blocking collectives, shards(): back = lax.all_to_all(back, 'member', 0, 0, tiled=True)  19.5 us
    ppermute x1, starting transfers between devices, shards(): before = lax.ppermute(tail, 'region', up)  3.88 us
    ppermute x1, waiting for transfers between devices, shards(): after = lax.ppermute(head, 'region', [(j, i) for i, j in up])  2.79 us
    pallas_call x1, Pallas kernels, shards(): pl.pallas_call(functools.partial(analyse_kernel, fields), out_shape=jax.S...  2.25 us
  transfers between devices with their start and end apart: 2, of which 1 were waited for; matrix products, arithmetic and copies ran while one was open for 0% of the time, Pallas kernels for 0%

profile of v4, /device:TPU:193, one launch (start us, length us, event | category | flops | bytes accessed | tf_op | source)
XLA Modules:
  0.0 60.1 jit_solution(7588051999909619341)
XLA Ops:
  0.0 0.8 %pad_maximum_fusion = (bf16[9,3,128]{2,1,0:T(4,128)(2,1)S(1)}, bf16[9,3,128]{2,1,0:T(4,128)(2,1)S(1)}) fusion(bf16[1,32,128]{2,1,0:T(8,128)(2,1)} %bitcast.6, bf16[8,32,128]{2,1,0:T(8,128)(2,1)} %anomalies_ref.1), kind=kLoop, calls=%fused_computation | loop fusion | flops 27648 | bytes 87552 | tf_op jit(solution)/shard_map/concatenate | solution.py:149
  0.8 0.0 copy-start
  0.8 0.0 copy-start.1
  0.8 0.0 copy-start.2
  0.8 3.9 %collective-permute-start = (bf16[9,3,128]{2,1,0:T(4,128)(2,1)S(1)}, bf16[9,3,128]{2,1,0:T(4,128)(2,1)S(1)}, u32[]{:S(2)}, u32[]{:S(2)}) collective-permute-start(bf16[9,3,128]{2,1,0:T(4,128)(2,1)S(1)} %get-tuple-element.13), channel_id=1, source_target_pairs={{0,1},{1,2},{2,3},{3,4},{4,5},{5,6},{6,7},{7,8},{8,9},{9,10},{10,1... | collective-permute-start | bytes 20744 | tf_op jit(solution)/shard_map/ppermute | solution.py:161
  4.7 0.0 collective-permute-start.1
  4.7 0.0 copy-start.3
  5.4 0.0 copy-start.4
  5.4 0.0 copy-done
  5.4 0.0 copy-done.1
  5.4 0.0 copy-done.2
  5.4 0.0 copy-done.3
  5.4 0.6 %copy-done.4 = s32[32,4]{0,1:T(4,128)S(1)} copy-done((s32[32,4]{0,1:T(4,128)S(1)}, s32[32,4]{0,1:T(4,128)}, u32[]{:S(2)}) %copy-start.4) | copy-done | bytes 536
  6.1 0.1 pack.1
  6.2 0.0 collective-permute-done.before_ref
  6.2 2.8 %collective-permute-done.1.after_ref = bf16[9,3,128]{2,1,0:T(4,128)(2,1)S(1)} collective-permute-done((bf16[9,3,128]{2,1,0:T(4,128)(2,1)S(1)}, bf16[9,3,128]{2,1,0:T(4,128)(2,1)S(1)}, u32[]{:S(2)}, u32[]{:S(2)}) %collective-permute-start.1) | collective-permute-done | bytes 6944 | tf_op jit(solution)/shard_map/ppermute | solution.py:162
  9.0 0.7 %choose.1 = (bf16[32,10,8,128]{3,2,1,0:T(8,128)(2,1)S(1)}, f32[8,512]{1,0:T(8,128)S(1)}) custom-call(s32[1]{0:T(128)S(6)} %add.3.place_ref, s32[4,32]{1,0:T(4,128)S(1)} %bitcast.8, bf16[32,6,8,128]{3,2,1,0:T(8,128)(2,1)S(1)} %get-tuple-element.11.packed_ref, bf16[32,8,128]{2,1,0:T(8,128)(2,1)S(1)} %get-tuple-element.12.blocks_ref, ...), custom_call_target="tpu_custom_call" | custom-call | tf_op jit(solution)/shard_map/choose/pallas_call | solution.py:176
  9.7 27.7 %all_to_all.10.incoming_ref = bf16[32,10,8,128]{3,2,1,0:T(8,128)(2,1)S(1)} all-to-all(bf16[32,10,8,128]{3,2,1,0:T(8,128)(2,1)S(1)} %get-tuple-element.15), channel_id=1, replica_groups=mesh['member'=32,'region'=16] {'member'}, dimensions={0} | all-to-all | bytes 1310720 | tf_op jit(solution)/shard_map/all_to_all | solution.py:191
  37.4 2.2 %analyse.1 = bf16[32,6,8,128]{3,2,1,0:T(8,128)(2,1)S(1)} custom-call(bf16[32,10,8,128]{3,2,1,0:T(8,128)(2,1)S(1)} %all_to_all.10.incoming_ref, f32[8,512]{1,0:T(8,128)S(1)} %get-tuple-element.16.side_ref), custom_call_target="tpu_custom_call" | custom-call | tf_op jit(solution)/shard_map/analyse/pallas_call | solution.py:192
  39.7 19.5 %all_to_all.11 = bf16[32,6,8,128]{3,2,1,0:T(8,128)(2,1)S(1)} all-to-all(bf16[32,6,8,128]{3,2,1,0:T(8,128)(2,1)S(1)} %analyse.1), channel_id=1, replica_groups=mesh['member'=32,'region'=16] {'member'}, dimensions={0} | all-to-all | bytes 786432 | tf_op jit(solution)/shard_map/all_to_all | solution.py:200
  59.2 0.8 %copy.7 = bf16[8,32,6,128]{3,1,2,0:T(8,128)(2,1)} copy(bf16[8,32,6,128]{3,0,2,1:T(8,128)(2,1)S(1)} %bitcast.9) | data formatting | bytes 786432 | tf_op jit(solution)/shard_map/transpose | solution.py:201
  (1 shorter events, 0.0 us)
Async XLA Ops:
  0.8 4.6 %copy-start = (bf16[8,32,6,128]{3,1,2,0:T(8,128)(2,1)S(1)}, bf16[8,32,6,128]{3,1,2,0:T(8,128)(2,1)}, u32[]{:S(2)}) copy-start(bf16[8,32,6,128]{3,1,2,0:T(8,128)(2,1)} %param.6) | copy-start | bytes 1179652
  0.8 4.6 %copy-start.1 = (f32[32,4,128]{2,1,0:T(4,128)S(1)}, f32[32,4,128]{2,1,0:T(4,128)}, u32[]{:S(2)}) copy-start(f32[32,4,128]{2,1,0:T(4,128)} %loc_ref.3) | copy-start | bytes 196612
  0.8 4.6 %copy-start.2 = (bf16[8,32,128]{2,1,0:T(8,128)(2,1)S(1)}, bf16[8,32,128]{2,1,0:T(8,128)(2,1)}, u32[]{:S(2)}) copy-start(bf16[8,32,128]{2,1,0:T(8,128)(2,1)} %anomalies_ref.1) | copy-start | bytes 196612
  0.8 5.4 %collective-permute-start = (bf16[9,3,128]{2,1,0:T(4,128)(2,1)S(1)}, bf16[9,3,128]{2,1,0:T(4,128)(2,1)S(1)}, u32[]{:S(2)}, u32[]{:S(2)}) collective-permute-start(bf16[9,3,128]{2,1,0:T(4,128)(2,1)S(1)} %get-tuple-element.13), channel_id=1, source_target_pairs={{0,1},{1,2},{2,3},{3,4},{4,5},{5,6},{6,7},{7,8},{8,9},{9,10},{10,1... | collective-permute-start | bytes 20744 | tf_op jit(solution)/shard_map/ppermute | solution.py:161
  4.7 4.3 %collective-permute-start.1 = (bf16[9,3,128]{2,1,0:T(4,128)(2,1)S(1)}, bf16[9,3,128]{2,1,0:T(4,128)(2,1)S(1)}, u32[]{:S(2)}, u32[]{:S(2)}) collective-permute-start(bf16[9,3,128]{2,1,0:T(4,128)(2,1)S(1)} %get-tuple-element.14), channel_id=1, source_target_pairs={{1,0},{2,1},{3,2},{4,3},{5,4},{6,5},{7,6},{8,7},{9,8},{10,9},{11,1... | collective-permute-start | bytes 20744 | tf_op jit(solution)/shard_map/ppermute | solution.py:162
  4.7 0.7 %copy-start.3 = (bf16[32,128]{1,0:T(8,128)(2,1)S(1)}, bf16[32,128]{1,0:T(8,128)(2,1)}, u32[]{:S(2)}) copy-start(bf16[32,128]{1,0:T(8,128)(2,1)} %misfit_ref.3) | copy-start | bytes 24580
  5.4 0.7 %copy-start.4 = (s32[32,4]{0,1:T(4,128)S(1)}, s32[32,4]{0,1:T(4,128)}, u32[]{:S(2)}) copy-start(s32[32,4]{0,1:T(4,128)} %param.10) | copy-start | bytes 1540

commit v5 on v4

--- a/solution.py
+++ b/solution.py
@@ -107,36 +107,54 @@
     head_out_ref[...] = head_ref[...]
 
 
-def pack_kernel(table_ref, loc_ref, misfit_ref, forecast_ref, anomalies_ref, out_ref, blocks_ref):
+def pack_kernel(
+    place_ref, table_ref, forecast_ref, anomalies_ref, loc_ref, misfit_ref,
+    out_ref, chosen_ref, marks_ref, side_ref, blocks_ref, line_ref
+):
+    count, obs = misfit_ref.shape
+    used, slots = table_ref.shape
     for field in range(forecast_ref.shape[1]):
         out_ref[:, field] = jnp.swapaxes(forecast_ref[:, field], 0, 1)
     blocks_ref[...] = jnp.swapaxes(anomalies_ref[...], 0, 1)
-
-
-def choose_kernel(
-    fields, place_ref, table_ref, packed_ref, blocks_ref, loc_ref, misfit_ref, before_ref, after_ref,
-    out_ref, side_ref, all_ref, line_ref
-):
-    count, members, obs = blocks_ref.shape
-    all_ref[HW : HW + count] = blocks_ref[...]
-    all_ref[:HW] = jnp.swapaxes(before_ref[:members], 0, 1)
-    all_ref[HW + count :] = jnp.swapaxes(after_ref[:members], 0, 1)
-    out_ref[:, :fields] = packed_ref[...]
-    used, slots = table_ref.shape
+    tile = marks_ref.shape[2:]
     for slot in range(slots):
         for h in range(used):
-            out_ref[slot, fields + h] = all_ref[table_ref[h, slot]]
+            index = table_ref[h, slot]
+            chosen_ref[slot, h] = blocks_ref[jnp.clip(index - HW, 0, count - 1)]
+            marks_ref[slot, h] = jnp.full(tile, index, jnp.int32).astype(marks_ref.dtype)
     dead = place_ref[0] >= slots
     me = jnp.where(dead, place_ref[0] - slots, place_ref[0])
-    line_ref[HW : HW + count] = misfit_ref[...].astype(jnp.float32)
-    line_ref[:HW] = before_ref[members].astype(jnp.float32)
-    line_ref[HW + count :] = after_ref[members].astype(jnp.float32)
+    line_ref[...] = misfit_ref[...].astype(jnp.float32)
     loc = loc_ref[me]
     side_ref[...] = jnp.full(side_ref.shape, jnp.where(dead, 0.0, 1.0), jnp.float32)
     for h in range(used):
         at = slice(h * obs, (h + 1) * obs)
+        index = table_ref[h, me]
         side_ref[0:1, at] = loc[h : h + 1]
-        side_ref[1:2, at] = line_ref[pl.ds(table_ref[h, me], 1)]
+        side_ref[1:2, at] = line_ref[pl.ds(jnp.clip(index - HW, 0, count - 1), 1)]
+        side_ref[3:4, at] = jnp.full((1, obs), index, jnp.int32).astype(jnp.float32)
+
+
+def choose_kernel(
+    fields, count, packed_ref, chosen_ref, marks_ref, rows_ref, before_ref, after_ref, out_ref, side_ref
+):
+    slots, used, members, obs = chosen_ref.shape
+    out_ref[:, :fields] = packed_ref[...]
+    ends = []
+    for ref, first in ((before_ref, 0), (after_ref, HW + count)):
+        edge = jnp.swapaxes(ref[:members], 0, 1)
+        line = ref[members].astype(jnp.float32)
+        ends += [(first + i, edge[i], line[i : i + 1]) for i in range(HW)]
+    for h in range(used):
+        marks, chosen = marks_ref[:, h], chosen_ref[:, h]
+        for index, block, _ in ends:
+            chosen = jnp.where(marks == jnp.bfloat16(index), block[None], chosen)
+        out_ref[:, fields + h] = chosen
+    side_ref[...] = rows_ref[...]
+    marks, innov = rows_ref[3:4], rows_ref[1:2]
+    for index, _, line in ends:
+        innov = jnp.where(marks == index, jnp.concatenate([line] * used, axis=1), innov)
+    side_ref[1:2] = innov
 
 
 def shards(forecast, anomalies, misfit, precision, table, tally):
@@ -160,34 +178,38 @@
     )(stacked[:, count - HW :], stacked[:, :HW])
     before = lax.ppermute(tail, "region", up)
     after = lax.ppermute(head, "region", [(j, i) for i, j in up])
-    packed, blocks = pl.pallas_call(
+    me = lax.axis_index("member").reshape(1)
+    place = me + slots * (me >= tally).astype(jnp.int32)
+    blocks = jax.ShapeDtypeStruct((slots, used, members, obs), anomalies.dtype)
+    rows = jax.ShapeDtypeStruct((8, used * obs), jnp.float32)
+    packed, chosen, marks, side = pl.pallas_call(
         pack_kernel,
         out_shape=(
             jax.ShapeDtypeStruct((slots, fields, members, cells), forecast.dtype),
-            jax.ShapeDtypeStruct((count, members, obs), anomalies.dtype),
+            blocks,
+            blocks,
+            rows,
         ),
-        in_specs=[VMEM] * 5,
-        out_specs=(VMEM, VMEM),
+        in_specs=[SMEM, SMEM] + [VMEM] * 4,
+        out_specs=(VMEM,) * 4,
+        scratch_shapes=[
+            pltpu.VMEM((count, members, obs), anomalies.dtype),
+            pltpu.VMEM((count, obs), jnp.float32),
+        ],
         compiler_params=PARAMS,
         name="pack",
-    )(table, precision, misfit, jnp.transpose(forecast, (0, 2, 1, 3)), anomalies)
-    me = lax.axis_index("member").reshape(1)
-    place = me + slots * (me >= tally).astype(jnp.int32)
+    )(place, table, jnp.transpose(forecast, (0, 2, 1, 3)), anomalies, precision, misfit)
     outgoing, side = pl.pallas_call(
-        functools.partial(choose_kernel, fields),
+        functools.partial(choose_kernel, fields, count),
         out_shape=(
             jax.ShapeDtypeStruct((slots, fields + used, members, cells), packed.dtype),
-            jax.ShapeDtypeStruct((8, used * obs), jnp.float32),
+            rows,
         ),
-        in_specs=[SMEM, SMEM] + [VMEM] * 6,
+        in_specs=[VMEM] * 6,
         out_specs=(VMEM, VMEM),
-        scratch_shapes=[
-            pltpu.VMEM((count + 2 * HW, members, obs), blocks.dtype),
-            pltpu.VMEM((count + 2 * HW, obs), jnp.float32),
-        ],
         compiler_params=PARAMS,
         name="choose",
-    )(place, table, packed, blocks, precision, misfit, before, after)
+    )(packed, chosen, marks, side, before, after)
     incoming = lax.all_to_all(outgoing, "member", 0, 0, tiled=True)
     back = pl.pallas_call(
         functools.partial(analyse_kernel, fields),

time: 60.4 us -> 60.1 us (level)
  the two profiles are of different devices: /device:TPU:193 before, /device:TPU:128 now
where the time goes in v5:
time: 60.1 us; the launch traced here: 59.8 us
  blocking collectives  51.5 us (86%)
  Pallas kernels  3.47 us (6%)
  starting transfers between devices  1.75 us (3%)
  local copies, waits for them, and re-layouts  1.51 us (3%)
  between operations  0.79 us (1%)
  other arithmetic  0.78 us (1%)
    all_to_all x1, blocking collectives, shards(): incoming = lax.all_to_all(outgoing, 'member', 0, 0, tiled=True)  30.5 us
    all_to_all x1, blocking collectives, shards(): back = lax.all_to_all(back, 'member', 0, 0, tiled=True)  21 us
    pallas_call x1, Pallas kernels, shards(): pl.pallas_call(functools.partial(analyse_kernel, fields), out_shape=jax.S...  2.25 us
    ppermute x1, starting transfers between devices, shards(): after = lax.ppermute(head, 'region', [(j, i) for i, j in up])  1.73 us
  transfers between devices with their start and end apart: 2, of which 0 were waited for; matrix products, arithmetic and copies ran while one was open for 0% of the time, Pallas kernels for 2%

profile of v5, /device:TPU:128, one launch (start us, length us, event | category | flops | bytes accessed | tf_op | source)
XLA Modules:
  0.0 59.8 jit_solution(4204290180946328808)
XLA Ops:
  0.0 0.8 %pad_maximum_fusion = (bf16[9,3,128]{2,1,0:T(4,128)(2,1)S(1)}, bf16[9,3,128]{2,1,0:T(4,128)(2,1)S(1)}) fusion(bf16[1,32,128]{2,1,0:T(8,128)(2,1)} %bitcast.6, bf16[8,32,128]{2,1,0:T(8,128)(2,1)} %anomalies_ref.1), kind=kLoop, calls=%fused_computation | loop fusion | flops 27648 | bytes 87552 | tf_op jit(solution)/shard_map/concatenate | solution.py:167
  0.8 0.0 copy-start
  0.8 0.0 copy-start.1
  0.8 0.0 copy-start.2
  0.8 0.0 collective-permute-start
  0.9 1.7 %collective-permute-start.1 = (bf16[9,3,128]{2,1,0:T(4,128)(2,1)S(1)}, bf16[9,3,128]{2,1,0:T(4,128)(2,1)S(1)}, u32[]{:S(2)}, u32[]{:S(2)}) collective-permute-start(bf16[9,3,128]{2,1,0:T(4,128)(2,1)S(1)} %get-tuple-element.18), channel_id=1, source_target_pairs={{1,0},{2,1},{3,2},{4,3},{5,4},{6,5},{7,6},{8,7},{9,8},{10,9},{11,1... | collective-permute-start | bytes 20744 | tf_op jit(solution)/shard_map/ppermute | solution.py:180
  2.6 0.0 copy-start.3
  3.3 0.0 copy-start.4
  3.3 0.0 copy-done
  3.3 0.0 copy-done.1
  3.3 0.0 copy-done.2
  3.3 0.0 copy-done.3
  3.3 0.6 %copy-done.4 = s32[32,4]{0,1:T(4,128)S(1)} copy-done((s32[32,4]{0,1:T(4,128)S(1)}, s32[32,4]{0,1:T(4,128)}, u32[]{:S(2)}) %copy-start.4) | copy-done | bytes 536
  4.0 1.0 %pack.1 = (bf16[32,6,8,128]{3,2,1,0:T(8,128)(2,1)S(1)}, bf16[32,4,8,128]{3,2,1,0:T(8,128)(2,1)S(1)}, bf16[32,4,8,128]{3,2,1,0:T(8,128)(2,1)S(1)}, f32[8,512]{1,0:T(8,128)S(1)}) custom-call(s32[1]{0:T(128)S(6)} %add.3.place_ref, s32[4,32]{1,0:T(4,128)S(1)} %bitcast.7, bf16[8,6,32,128]{3,2,1,0:T(8,128)(2,1)S(1)} %bitcast.5, bf16[8,32,128]{2,1,0:T(8,128)(2,1)S(1)} %copy-done.1, ...), custom_call_target="tpu_custom_call" | custom-call | tf_op jit(solution)/shard_map/pack/pallas_call | solution.py:185
  4.9 0.0 collective-permute-done.before_ref
  4.9 0.0 collective-permute-done.1.after_ref
  4.9 0.2 choose.1
  5.2 30.5 %all_to_all.10.incoming_ref = bf16[32,10,8,128]{3,2,1,0:T(8,128)(2,1)S(1)} all-to-all(bf16[32,10,8,128]{3,2,1,0:T(8,128)(2,1)S(1)} %get-tuple-element.19), channel_id=1, replica_groups=mesh['member'=32,'region'=16] {'member'}, dimensions={0} | all-to-all | bytes 1310720 | tf_op jit(solution)/shard_map/all_to_all | solution.py:213
  35.7 2.2 %analyse.1 = bf16[32,6,8,128]{3,2,1,0:T(8,128)(2,1)S(1)} custom-call(bf16[32,10,8,128]{3,2,1,0:T(8,128)(2,1)S(1)} %all_to_all.10.incoming_ref, f32[8,512]{1,0:T(8,128)S(1)} %get-tuple-element.20.side_ref), custom_call_target="tpu_custom_call" | custom-call | tf_op jit(solution)/shard_map/analyse/pallas_call | solution.py:214
  37.9 21.0 %all_to_all.11 = bf16[32,6,8,128]{3,2,1,0:T(8,128)(2,1)S(1)} all-to-all(bf16[32,6,8,128]{3,2,1,0:T(8,128)(2,1)S(1)} %analyse.1), channel_id=1, replica_groups=mesh['member'=32,'region'=16] {'member'}, dimensions={0} | all-to-all | bytes 786432 | tf_op jit(solution)/shard_map/all_to_all | solution.py:222
  59.0 0.8 %copy.7 = bf16[8,32,6,128]{3,1,2,0:T(8,128)(2,1)} copy(bf16[8,32,6,128]{3,0,2,1:T(8,128)(2,1)S(1)} %bitcast.8) | data formatting | bytes 786432 | tf_op jit(solution)/shard_map/transpose | solution.py:223
  (1 shorter events, 0.0 us)
Async XLA Ops:
  0.8 2.5 %copy-start = (bf16[8,32,6,128]{3,1,2,0:T(8,128)(2,1)S(1)}, bf16[8,32,6,128]{3,1,2,0:T(8,128)(2,1)}, u32[]{:S(2)}) copy-start(bf16[8,32,6,128]{3,1,2,0:T(8,128)(2,1)} %param.6) | copy-start | bytes 1179652
  0.8 2.5 %copy-start.1 = (bf16[8,32,128]{2,1,0:T(8,128)(2,1)S(1)}, bf16[8,32,128]{2,1,0:T(8,128)(2,1)}, u32[]{:S(2)}) copy-start(bf16[8,32,128]{2,1,0:T(8,128)(2,1)} %anomalies_ref.1) | copy-start | bytes 196612
  0.8 2.5 %copy-start.2 = (f32[32,4,128]{2,1,0:T(4,128)S(1)}, f32[32,4,128]{2,1,0:T(4,128)}, u32[]{:S(2)}) copy-start(f32[32,4,128]{2,1,0:T(4,128)} %loc_ref.1) | copy-start | bytes 196612
  0.8 4.1 %collective-permute-start = (bf16[9,3,128]{2,1,0:T(4,128)(2,1)S(1)}, bf16[9,3,128]{2,1,0:T(4,128)(2,1)S(1)}, u32[]{:S(2)}, u32[]{:S(2)}) collective-permute-start(bf16[9,3,128]{2,1,0:T(4,128)(2,1)S(1)} %get-tuple-element.17), channel_id=1, source_target_pairs={{0,1},{1,2},{2,3},{3,4},{4,5},{5,6},{6,7},{7,8},{8,9},{9,10},{10,1... | collective-permute-start | bytes 20744 | tf_op jit(solution)/shard_map/ppermute | solution.py:179
  0.9 4.1 %collective-permute-start.1 = (bf16[9,3,128]{2,1,0:T(4,128)(2,1)S(1)}, bf16[9,3,128]{2,1,0:T(4,128)(2,1)S(1)}, u32[]{:S(2)}, u32[]{:S(2)}) collective-permute-start(bf16[9,3,128]{2,1,0:T(4,128)(2,1)S(1)} %get-tuple-element.18), channel_id=1, source_target_pairs={{1,0},{2,1},{3,2},{4,3},{5,4},{6,5},{7,6},{8,7},{9,8},{10,9},{11,1... | collective-permute-start | bytes 20744 | tf_op jit(solution)/shard_map/ppermute | solution.py:180
  2.6 0.7 %copy-start.3 = (bf16[32,128]{1,0:T(8,128)(2,1)S(1)}, bf16[32,128]{1,0:T(8,128)(2,1)}, u32[]{:S(2)}) copy-start(bf16[32,128]{1,0:T(8,128)(2,1)} %misfit_ref.1) | copy-start | bytes 24580
  3.3 0.7 %copy-start.4 = (s32[32,4]{0,1:T(4,128)S(1)}, s32[32,4]{0,1:T(4,128)}, u32[]{:S(2)}) copy-start(s32[32,4]{0,1:T(4,128)} %param.10) | copy-start | bytes 1540

commit v6 on v5

--- a/solution.py
+++ b/solution.py
@@ -108,28 +108,31 @@
 
 
 def pack_kernel(
-    place_ref, table_ref, forecast_ref, anomalies_ref, loc_ref, misfit_ref,
+    me_ref, table_ref, forecast_ref, anomalies_ref, loc_ref, misfit_ref,
     out_ref, chosen_ref, marks_ref, side_ref, blocks_ref, line_ref
 ):
     count, obs = misfit_ref.shape
-    used, slots = table_ref.shape
+    used, slots = table_ref.shape[0] - 1, table_ref.shape[1]
     for field in range(forecast_ref.shape[1]):
         out_ref[:, field] = jnp.swapaxes(forecast_ref[:, field], 0, 1)
     blocks_ref[...] = jnp.swapaxes(anomalies_ref[...], 0, 1)
     tile = marks_ref.shape[2:]
+    table = table_ref[...]
     for slot in range(slots):
         for h in range(used):
-            index = table_ref[h, slot]
+            index = table[h, slot]
             chosen_ref[slot, h] = blocks_ref[jnp.clip(index - HW, 0, count - 1)]
             marks_ref[slot, h] = jnp.full(tile, index, jnp.int32).astype(marks_ref.dtype)
-    dead = place_ref[0] >= slots
-    me = jnp.where(dead, place_ref[0] - slots, place_ref[0])
+    me = me_ref[0]
+    dead = me >= table[used, 0]
+    lane = lax.broadcasted_iota(jnp.int32, table.shape, 1)
+    mine = jnp.sum(jnp.where(lane == me, table, 0), axis=1, keepdims=True)
     line_ref[...] = misfit_ref[...].astype(jnp.float32)
     loc = loc_ref[me]
     side_ref[...] = jnp.full(side_ref.shape, jnp.where(dead, 0.0, 1.0), jnp.float32)
     for h in range(used):
         at = slice(h * obs, (h + 1) * obs)
-        index = table_ref[h, me]
+        index = mine[h, 0]
         side_ref[0:1, at] = loc[h : h + 1]
         side_ref[1:2, at] = line_ref[pl.ds(jnp.clip(index - HW, 0, count - 1), 1)]
         side_ref[3:4, at] = jnp.full((1, obs), index, jnp.int32).astype(jnp.float32)
@@ -179,7 +182,7 @@
     before = lax.ppermute(tail, "region", up)
     after = lax.ppermute(head, "region", [(j, i) for i, j in up])
     me = lax.axis_index("member").reshape(1)
-    place = me + slots * (me >= tally).astype(jnp.int32)
+    table = jnp.concatenate([table, jnp.broadcast_to(tally[None], (1, slots))], axis=0)
     blocks = jax.ShapeDtypeStruct((slots, used, members, obs), anomalies.dtype)
     rows = jax.ShapeDtypeStruct((8, used * obs), jnp.float32)
     packed, chosen, marks, side = pl.pallas_call(
@@ -190,7 +193,7 @@
             blocks,
             rows,
         ),
-        in_specs=[SMEM, SMEM] + [VMEM] * 4,
+        in_specs=[SMEM] + [VMEM] * 5,
         out_specs=(VMEM,) * 4,
         scratch_shapes=[
             pltpu.VMEM((count, members, obs), anomalies.dtype),
@@ -198,7 +201,7 @@
         ],
         compiler_params=PARAMS,
         name="pack",
-    )(place, table, jnp.transpose(forecast, (0, 2, 1, 3)), anomalies, precision, misfit)
+    )(me, table, jnp.transpose(forecast, (0, 2, 1, 3)), anomalies, precision, misfit)
     outgoing, side = pl.pallas_call(
         functools.partial(choose_kernel, fields, count),
         out_shape=(

time: 60.1 us -> 59.9 us (level)
  the two profiles are of different devices: /device:TPU:128 before, /device:TPU:193 now
where the time goes in v6:
time: 59.9 us; the launch traced here: 59.6 us
  blocking collectives  47.2 us (79%)
  starting transfers between devices  3.88 us (6%)
  waiting for transfers between devices  3.11 us (5%)
  Pallas kernels  2.94 us (5%)
  local copies, waits for them, and re-layouts  0.88 us (1%)
  between operations  0.79 us (1%)
  other arithmetic  0.78 us (1%)
    all_to_all x1, blocking collectives, shards(): incoming = lax.all_to_all(outgoing, 'member', 0, 0, tiled=True)  27.7 us
    all_to_all x1, blocking collectives, shards(): back = lax.all_to_all(back, 'member', 0, 0, tiled=True)  19.5 us
    ppermute x1, starting transfers between devices, shards(): before = lax.ppermute(tail, 'region', up)  3.88 us
    ppermute x1, waiting for transfers between devices, shards(): after = lax.ppermute(head, 'region', [(j, i) for i, j in up])  3.11 us
    pallas_call x1, Pallas kernels, shards(): pl.pallas_call(functools.partial(analyse_kernel, fields), out_shape=jax.S...  2.25 us
  transfers between devices with their start and end apart: 2, of which 1 were waited for; matrix products, arithmetic and copies ran while one was open for 0% of the time, Pallas kernels for 1%

profile of v6, /device:TPU:193, one launch (start us, length us, event | category | flops | bytes accessed | tf_op | source)
XLA Modules:
  0.0 59.6 jit_solution(11959958650072539225)
XLA Ops:
  0.0 0.8 %pad_maximum_fusion = (bf16[9,3,128]{2,1,0:T(4,128)(2,1)S(1)}, bf16[9,3,128]{2,1,0:T(4,128)(2,1)S(1)}) fusion(bf16[1,32,128]{2,1,0:T(8,128)(2,1)} %bitcast.8, bf16[8,32,128]{2,1,0:T(8,128)(2,1)} %anomalies_ref.1), kind=kLoop, calls=%fused_computation | loop fusion | flops 27648 | bytes 87552 | tf_op jit(solution)/shard_map/concatenate | solution.py:170
  0.8 0.0 copy-start.4
  0.8 0.0 copy-start
  0.8 0.0 copy-start.1
  0.8 0.0 copy-start.2
  0.8 3.9 %collective-permute-start = (bf16[9,3,128]{2,1,0:T(4,128)(2,1)S(1)}, bf16[9,3,128]{2,1,0:T(4,128)(2,1)S(1)}, u32[]{:S(2)}, u32[]{:S(2)}) collective-permute-start(bf16[9,3,128]{2,1,0:T(4,128)(2,1)S(1)} %get-tuple-element.17), channel_id=1, source_target_pairs={{0,1},{1,2},{2,3},{3,4},{4,5},{5,6},{6,7},{7,8},{8,9},{9,10},{10,1... | collective-permute-start | bytes 20744 | tf_op jit(solution)/shard_map/ppermute | solution.py:182
  4.7 0.0 collective-permute-start.1
  4.7 0.0 copy-start.3
  5.4 0.0 copy-done.4
  5.4 0.0 copy-done
  5.4 0.0 copy-done.1
  5.4 0.0 copy-done.2
  5.5 0.0 copy-done.3
  5.5 0.4 pack.1
  5.9 0.0 collective-permute-done.before_ref
  5.9 3.1 %collective-permute-done.1.after_ref = bf16[9,3,128]{2,1,0:T(4,128)(2,1)S(1)} collective-permute-done((bf16[9,3,128]{2,1,0:T(4,128)(2,1)S(1)}, bf16[9,3,128]{2,1,0:T(4,128)(2,1)S(1)}, u32[]{:S(2)}, u32[]{:S(2)}) %collective-permute-start.1) | collective-permute-done | bytes 6944 | tf_op jit(solution)/shard_map/ppermute | solution.py:183
  9.0 0.2 choose.1
  9.3 27.7 %all_to_all.10.incoming_ref = bf16[32,10,8,128]{3,2,1,0:T(8,128)(2,1)S(1)} all-to-all(bf16[32,10,8,128]{3,2,1,0:T(8,128)(2,1)S(1)} %get-tuple-element.19), channel_id=1, replica_groups=mesh['member'=32,'region'=16] {'member'}, dimensions={0} | all-to-all | bytes 1310720 | tf_op jit(solution)/shard_map/all_to_all | solution.py:216
  37.0 2.2 %analyse.1 = bf16[32,6,8,128]{3,2,1,0:T(8,128)(2,1)S(1)} custom-call(bf16[32,10,8,128]{3,2,1,0:T(8,128)(2,1)S(1)} %all_to_all.10.incoming_ref, f32[8,512]{1,0:T(8,128)S(1)} %get-tuple-element.20.side_ref), custom_call_target="tpu_custom_call" | custom-call | tf_op jit(solution)/shard_map/analyse/pallas_call | solution.py:217
  39.2 19.5 %all_to_all.11 = bf16[32,6,8,128]{3,2,1,0:T(8,128)(2,1)S(1)} all-to-all(bf16[32,6,8,128]{3,2,1,0:T(8,128)(2,1)S(1)} %analyse.1), channel_id=1, replica_groups=mesh['member'=32,'region'=16] {'member'}, dimensions={0} | all-to-all | bytes 786432 | tf_op jit(solution)/shard_map/all_to_all | solution.py:225
  58.8 0.8 %copy.7 = bf16[8,32,6,128]{3,1,2,0:T(8,128)(2,1)} copy(bf16[8,32,6,128]{3,0,2,1:T(8,128)(2,1)S(1)} %bitcast.9) | data formatting | bytes 786432 | tf_op jit(solution)/shard_map/transpose | solution.py:226
  (2 shorter events, 0.0 us)
Async XLA Ops:
  0.8 4.6 %copy-start.4 = (s32[32,4]{0,1:T(4,128)S(1)}, s32[32,4]{0,1:T(4,128)}, u32[]{:S(2)}) copy-start(s32[32,4]{0,1:T(4,128)} %param.10) | copy-start | bytes 1540
  0.8 4.6 %copy-start = (bf16[8,32,6,128]{3,1,2,0:T(8,128)(2,1)S(1)}, bf16[8,32,6,128]{3,1,2,0:T(8,128)(2,1)}, u32[]{:S(2)}) copy-start(bf16[8,32,6,128]{3,1,2,0:T(8,128)(2,1)} %param.6) | copy-start | bytes 1179652
  0.8 4.6 %copy-start.1 = (bf16[8,32,128]{2,1,0:T(8,128)(2,1)S(1)}, bf16[8,32,128]{2,1,0:T(8,128)(2,1)}, u32[]{:S(2)}) copy-start(bf16[8,32,128]{2,1,0:T(8,128)(2,1)} %anomalies_ref.1) | copy-start | bytes 196612
  0.8 4.6 %copy-start.2 = (f32[32,4,128]{2,1,0:T(4,128)S(1)}, f32[32,4,128]{2,1,0:T(4,128)}, u32[]{:S(2)}) copy-start(f32[32,4,128]{2,1,0:T(4,128)} %loc_ref.1) | copy-start | bytes 196612
  0.8 5.1 %collective-permute-start = (bf16[9,3,128]{2,1,0:T(4,128)(2,1)S(1)}, bf16[9,3,128]{2,1,0:T(4,128)(2,1)S(1)}, u32[]{:S(2)}, u32[]{:S(2)}) collective-permute-start(bf16[9,3,128]{2,1,0:T(4,128)(2,1)S(1)} %get-tuple-element.17), channel_id=1, source_target_pairs={{0,1},{1,2},{2,3},{3,4},{4,5},{5,6},{6,7},{7,8},{8,9},{9,10},{10,1... | collective-permute-start | bytes 20744 | tf_op jit(solution)/shard_map/ppermute | solution.py:182
  4.7 4.3 %collective-permute-start.1 = (bf16[9,3,128]{2,1,0:T(4,128)(2,1)S(1)}, bf16[9,3,128]{2,1,0:T(4,128)(2,1)S(1)}, u32[]{:S(2)}, u32[]{:S(2)}) collective-permute-start(bf16[9,3,128]{2,1,0:T(4,128)(2,1)S(1)} %get-tuple-element.18), channel_id=1, source_target_pairs={{1,0},{2,1},{3,2},{4,3},{5,4},{6,5},{7,6},{8,7},{9,8},{10,9},{11,1... | collective-permute-start | bytes 20744 | tf_op jit(solution)/shard_map/ppermute | solution.py:183
  4.7 0.7 %copy-start.3 = (bf16[32,128]{1,0:T(8,128)(2,1)S(1)}, bf16[32,128]{1,0:T(8,128)(2,1)}, u32[]{:S(2)}) copy-start(bf16[32,128]{1,0:T(8,128)(2,1)} %misfit_ref.1) | copy-start | bytes 24580

commit v7 on v6

--- a/solution.py
+++ b/solution.py
@@ -181,7 +181,9 @@
     )(stacked[:, count - HW :], stacked[:, :HW])
     before = lax.ppermute(tail, "region", up)
     after = lax.ppermute(head, "region", [(j, i) for i, j in up])
+    order = [ranks - 1 - i for i in range(ranks)]
     me = lax.axis_index("member").reshape(1)
+    me = ranks - 1 - me
     table = jnp.concatenate([table, jnp.broadcast_to(tally[None], (1, slots))], axis=0)
     blocks = jax.ShapeDtypeStruct((slots, used, members, obs), anomalies.dtype)
     rows = jax.ShapeDtypeStruct((8, used * obs), jnp.float32)
@@ -213,7 +215,7 @@
         compiler_params=PARAMS,
         name="choose",
     )(packed, chosen, marks, side, before, after)
-    incoming = lax.all_to_all(outgoing, "member", 0, 0, tiled=True)
+    incoming = lax.all_to_all(outgoing, "member", 0, 0, tiled=True, axis_index_groups=[order])
     back = pl.pallas_call(
         functools.partial(analyse_kernel, fields),
         out_shape=jax.ShapeDtypeStruct((ranks, fields, members, cells), forecast.dtype),
@@ -222,7 +224,7 @@
         compiler_params=PARAMS,
         name="analyse",
     )(incoming, side)
-    back = lax.all_to_all(back, "member", 0, 0, tiled=True)
+    back = lax.all_to_all(back, "member", 0, 0, tiled=True, axis_index_groups=[order])
     return jnp.transpose(back, (2, 0, 1, 3))
 
 

time: 59.9 us -> 57.1 us (0.953)
  the two profiles are of different devices: /device:TPU:193 before, /device:TPU:201 now
where the time goes in v7:
time: 57.1 us; the launch traced here: 56.8 us
  blocking collectives  44.4 us (78%)
  starting transfers between devices  3.88 us (7%)
  Pallas kernels  2.93 us (5%)
  waiting for transfers between devices  2.5 us (4%)
  local copies, waits for them, and re-layouts  1.52 us (3%)
  other arithmetic  0.78 us (1%)
  between operations  0.77 us (1%)
    all_to_all x1, blocking collectives, shards(): lax.all_to_all(outgoing, 'member', 0, 0, tiled=True, axis_index_groups=[o...  24.8 us
    all_to_all x1, blocking collectives, shards(): lax.all_to_all(back, 'member', 0, 0, tiled=True, axis_index_groups=[order])  19.6 us
    ppermute x1, starting transfers between devices, shards(): before = lax.ppermute(tail, 'region', up)  3.88 us
    ppermute x1, waiting for transfers between devices, shards(): after = lax.ppermute(head, 'region', [(j, i) for i, j in up])  2.5 us
    pallas_call x1, Pallas kernels, shards(): pl.pallas_call(functools.partial(analyse_kernel, fields), out_shape=jax.S...  2.25 us
  transfers between devices with their start and end apart: 2, of which 1 were waited for; matrix products, arithmetic and copies ran while one was open for 0% of the time, Pallas kernels for 1%

profile of v7, /device:TPU:201, one launch (start us, length us, event | category | flops | bytes accessed | tf_op | source)
XLA Modules:
  0.0 56.8 jit_solution(6973444323139461513)
XLA Ops:
  0.0 0.8 %pad_maximum_fusion = (bf16[9,3,128]{2,1,0:T(4,128)(2,1)S(1)}, bf16[9,3,128]{2,1,0:T(4,128)(2,1)S(1)}) fusion(bf16[1,32,128]{2,1,0:T(8,128)(2,1)} %bitcast.8, bf16[8,32,128]{2,1,0:T(8,128)(2,1)} %anomalies_ref.1), kind=kLoop, calls=%fused_computation | loop fusion | flops 27648 | bytes 87552 | tf_op jit(solution)/shard_map/concatenate | solution.py:170
  0.8 0.0 copy-start.4
  0.8 0.0 copy-start
  0.8 0.0 copy-start.1
  0.8 0.0 copy-start.2
  0.8 3.9 %collective-permute-start = (bf16[9,3,128]{2,1,0:T(4,128)(2,1)S(1)}, bf16[9,3,128]{2,1,0:T(4,128)(2,1)S(1)}, u32[]{:S(2)}, u32[]{:S(2)}) collective-permute-start(bf16[9,3,128]{2,1,0:T(4,128)(2,1)S(1)} %get-tuple-element.17), channel_id=1, source_target_pairs={{0,1},{1,2},{2,3},{3,4},{4,5},{5,6},{6,7},{7,8},{8,9},{9,10},{10,1... | collective-permute-start | bytes 20744 | tf_op jit(solution)/shard_map/ppermute | solution.py:182
  4.7 0.0 collective-permute-start.1
  5.4 0.0 copy-start.3
  5.4 0.0 copy-done.4
  5.4 0.0 copy-done
  5.4 0.0 copy-done.1
  5.4 0.0 copy-done.2
  5.4 0.6 %copy-done.3 = bf16[32,128]{1,0:T(8,128)(2,1)S(1)} copy-done((bf16[32,128]{1,0:T(8,128)(2,1)S(1)}, bf16[32,128]{1,0:T(8,128)(2,1)}, u32[]{:S(2)}) %copy-start.3) | copy-done | bytes 8216
  6.1 0.4 pack.1
  6.5 0.0 collective-permute-done.before_ref
  6.5 2.5 %collective-permute-done.1.after_ref = bf16[9,3,128]{2,1,0:T(4,128)(2,1)S(1)} collective-permute-done((bf16[9,3,128]{2,1,0:T(4,128)(2,1)S(1)}, bf16[9,3,128]{2,1,0:T(4,128)(2,1)S(1)}, u32[]{:S(2)}, u32[]{:S(2)}) %collective-permute-start.1) | collective-permute-done | bytes 6944 | tf_op jit(solution)/shard_map/ppermute | solution.py:183
  9.0 0.2 choose.1
  9.3 24.8 %all_to_all.10.incoming_ref = bf16[32,10,8,128]{3,2,1,0:T(8,128)(2,1)S(1)} all-to-all(bf16[32,10,8,128]{3,2,1,0:T(8,128)(2,1)S(1)} %get-tuple-element.19), channel_id=1, replica_groups={{496,480,464,448,432,416,400,384,368,352,336,320,304,288,272,256,240,22..., dimensions={0} | all-to-all | bytes 1310720 | tf_op jit(solution)/shard_map/all_to_all | solution.py:218
  34.1 2.2 %analyse.1 = bf16[32,6,8,128]{3,2,1,0:T(8,128)(2,1)S(1)} custom-call(bf16[32,10,8,128]{3,2,1,0:T(8,128)(2,1)S(1)} %all_to_all.10.incoming_ref, f32[8,512]{1,0:T(8,128)S(1)} %get-tuple-element.20.side_ref), custom_call_target="tpu_custom_call" | custom-call | tf_op jit(solution)/shard_map/analyse/pallas_call | solution.py:219
  36.3 19.6 %all_to_all.11 = bf16[32,6,8,128]{3,2,1,0:T(8,128)(2,1)S(1)} all-to-all(bf16[32,6,8,128]{3,2,1,0:T(8,128)(2,1)S(1)} %analyse.1), channel_id=1, replica_groups={{496,480,464,448,432,416,400,384,368,352,336,320,304,288,272,256,240,22..., dimensions={0} | all-to-all | bytes 786432 | tf_op jit(solution)/shard_map/all_to_all | solution.py:227
  56.0 0.8 %copy.7 = bf16[8,32,6,128]{3,1,2,0:T(8,128)(2,1)} copy(bf16[8,32,6,128]{3,0,2,1:T(8,128)(2,1)S(1)} %bitcast.9) | data formatting | bytes 786432 | tf_op jit(solution)/shard_map/transpose | solution.py:228
  (2 shorter events, 0.0 us)
Async XLA Ops:
  0.8 4.6 %copy-start.4 = (s32[32,4]{0,1:T(4,128)S(1)}, s32[32,4]{0,1:T(4,128)}, u32[]{:S(2)}) copy-start(s32[32,4]{0,1:T(4,128)} %param.10) | copy-start | bytes 1540
  0.8 4.6 %copy-start = (bf16[8,32,6,128]{3,1,2,0:T(8,128)(2,1)S(1)}, bf16[8,32,6,128]{3,1,2,0:T(8,128)(2,1)}, u32[]{:S(2)}) copy-start(bf16[8,32,6,128]{3,1,2,0:T(8,128)(2,1)} %param.6) | copy-start | bytes 1179652
  0.8 4.6 %copy-start.1 = (bf16[8,32,128]{2,1,0:T(8,128)(2,1)S(1)}, bf16[8,32,128]{2,1,0:T(8,128)(2,1)}, u32[]{:S(2)}) copy-start(bf16[8,32,128]{2,1,0:T(8,128)(2,1)} %anomalies_ref.1) | copy-start | bytes 196612
  0.8 4.6 %copy-start.2 = (f32[32,4,128]{2,1,0:T(4,128)S(1)}, f32[32,4,128]{2,1,0:T(4,128)}, u32[]{:S(2)}) copy-start(f32[32,4,128]{2,1,0:T(4,128)} %loc_ref.1) | copy-start | bytes 196612
  0.8 5.7 %collective-permute-start = (bf16[9,3,128]{2,1,0:T(4,128)(2,1)S(1)}, bf16[9,3,128]{2,1,0:T(4,128)(2,1)S(1)}, u32[]{:S(2)}, u32[]{:S(2)}) collective-permute-start(bf16[9,3,128]{2,1,0:T(4,128)(2,1)S(1)} %get-tuple-element.17), channel_id=1, source_target_pairs={{0,1},{1,2},{2,3},{3,4},{4,5},{5,6},{6,7},{7,8},{8,9},{9,10},{10,1... | collective-permute-start | bytes 20744 | tf_op jit(solution)/shard_map/ppermute | solution.py:182
  4.7 4.3 %collective-permute-start.1 = (bf16[9,3,128]{2,1,0:T(4,128)(2,1)S(1)}, bf16[9,3,128]{2,1,0:T(4,128)(2,1)S(1)}, u32[]{:S(2)}, u32[]{:S(2)}) collective-permute-start(bf16[9,3,128]{2,1,0:T(4,128)(2,1)S(1)} %get-tuple-element.18), channel_id=1, source_target_pairs={{1,0},{2,1},{3,2},{4,3},{5,4},{6,5},{7,6},{8,7},{9,8},{10,9},{11,1... | collective-permute-start | bytes 20744 | tf_op jit(solution)/shard_map/ppermute | solution.py:183
  5.4 0.7 %copy-start.3 = (bf16[32,128]{1,0:T(8,128)(2,1)S(1)}, bf16[32,128]{1,0:T(8,128)(2,1)}, u32[]{:S(2)}) copy-start(bf16[32,128]{1,0:T(8,128)(2,1)} %misfit_ref.1) | copy-start | bytes 24580

commit v8 on v7

--- a/solution.py
+++ b/solution.py
@@ -181,9 +181,9 @@
     )(stacked[:, count - HW :], stacked[:, :HW])
     before = lax.ppermute(tail, "region", up)
     after = lax.ppermute(head, "region", [(j, i) for i, j in up])
-    order = [ranks - 1 - i for i in range(ranks)]
+    order = [(27 - i) % ranks for i in range(ranks)]
     me = lax.axis_index("member").reshape(1)
-    me = ranks - 1 - me
+    me = (27 - me + ranks) % ranks
     table = jnp.concatenate([table, jnp.broadcast_to(tally[None], (1, slots))], axis=0)
     blocks = jax.ShapeDtypeStruct((slots, used, members, obs), anomalies.dtype)
     rows = jax.ShapeDtypeStruct((8, used * obs), jnp.float32)

time: 57.1 us -> 55.7 us (0.975)
  the two profiles are of different devices: /device:TPU:201 before, /device:TPU:193 now
where the time goes in v8:
time: 55.7 us; the launch traced here: 55.3 us
  blocking collectives  42.9 us (77%)
  starting transfers between devices  3.88 us (7%)
  Pallas kernels  2.93 us (5%)
  waiting for transfers between devices  2.5 us (4%)
  local copies, waits for them, and re-layouts  1.51 us (3%)
  other arithmetic  0.78 us (1%)
  between operations  0.78 us (1%)
    all_to_all x1, blocking collectives, shards(): lax.all_to_all(outgoing, 'member', 0, 0, tiled=True, axis_index_groups=[o...  24.2 us
    all_to_all x1, blocking collectives, shards(): lax.all_to_all(back, 'member', 0, 0, tiled=True, axis_index_groups=[order])  18.8 us
    ppermute x1, starting transfers between devices, shards(): before = lax.ppermute(tail, 'region', up)  3.88 us
    ppermute x1, waiting for transfers between devices, shards(): after = lax.ppermute(head, 'region', [(j, i) for i, j in up])  2.5 us
    pallas_call x1, Pallas kernels, shards(): pl.pallas_call(functools.partial(analyse_kernel, fields), out_shape=jax.S...  2.25 us
  transfers between devices with their start and end apart: 2, of which 1 were waited for; matrix products, arithmetic and copies ran while one was open for 0% of the time, Pallas kernels for 1%

profile of v8, /device:TPU:193, one launch (start us, length us, event | category | flops | bytes accessed | tf_op | source)
XLA Modules:
  0.0 55.3 jit_solution(13341544805566014595)
XLA Ops:
  0.0 0.8 %pad_maximum_fusion = (bf16[9,3,128]{2,1,0:T(4,128)(2,1)S(1)}, bf16[9,3,128]{2,1,0:T(4,128)(2,1)S(1)}) fusion(bf16[1,32,128]{2,1,0:T(8,128)(2,1)} %bitcast.8, bf16[8,32,128]{2,1,0:T(8,128)(2,1)} %anomalies_ref.1), kind=kLoop, calls=%fused_computation | loop fusion | flops 27648 | bytes 87552 | tf_op jit(solution)/shard_map/concatenate | solution.py:170
  0.8 0.0 copy-start.4
  0.8 0.0 copy-start
  0.8 0.0 copy-start.1
  0.8 0.0 copy-start.2
  0.8 3.9 %collective-permute-start = (bf16[9,3,128]{2,1,0:T(4,128)(2,1)S(1)}, bf16[9,3,128]{2,1,0:T(4,128)(2,1)S(1)}, u32[]{:S(2)}, u32[]{:S(2)}) collective-permute-start(bf16[9,3,128]{2,1,0:T(4,128)(2,1)S(1)} %get-tuple-element.17), channel_id=1, source_target_pairs={{0,1},{1,2},{2,3},{3,4},{4,5},{5,6},{6,7},{7,8},{8,9},{9,10},{10,1... | collective-permute-start | bytes 20744 | tf_op jit(solution)/shard_map/ppermute | solution.py:182
  4.7 0.0 collective-permute-start.1
  5.4 0.0 copy-start.3
  5.4 0.0 copy-done.4
  5.4 0.0 copy-done
  5.4 0.0 copy-done.1
  5.4 0.0 copy-done.2
  5.5 0.6 %copy-done.3 = bf16[32,128]{1,0:T(8,128)(2,1)S(1)} copy-done((bf16[32,128]{1,0:T(8,128)(2,1)S(1)}, bf16[32,128]{1,0:T(8,128)(2,1)}, u32[]{:S(2)}) %copy-start.3) | copy-done | bytes 8216
  6.1 0.4 pack.1
  6.5 0.0 collective-permute-done.before_ref
  6.5 2.5 %collective-permute-done.1.after_ref = bf16[9,3,128]{2,1,0:T(4,128)(2,1)S(1)} collective-permute-done((bf16[9,3,128]{2,1,0:T(4,128)(2,1)S(1)}, bf16[9,3,128]{2,1,0:T(4,128)(2,1)S(1)}, u32[]{:S(2)}, u32[]{:S(2)}) %collective-permute-start.1) | collective-permute-done | bytes 6944 | tf_op jit(solution)/shard_map/ppermute | solution.py:183
  9.0 0.2 choose.1
  9.3 24.2 %all_to_all.10.incoming_ref = bf16[32,10,8,128]{3,2,1,0:T(8,128)(2,1)S(1)} all-to-all(bf16[32,10,8,128]{3,2,1,0:T(8,128)(2,1)S(1)} %get-tuple-element.19), channel_id=1, replica_groups={{432,416,400,384,368,352,336,320,304,288,272,256,240,224,208,192,176,16..., dimensions={0} | all-to-all | bytes 1310720 | tf_op jit(solution)/shard_map/all_to_all | solution.py:218
  33.5 2.2 %analyse.1 = bf16[32,6,8,128]{3,2,1,0:T(8,128)(2,1)S(1)} custom-call(bf16[32,10,8,128]{3,2,1,0:T(8,128)(2,1)S(1)} %all_to_all.10.incoming_ref, f32[8,512]{1,0:T(8,128)S(1)} %get-tuple-element.20.side_ref), custom_call_target="tpu_custom_call" | custom-call | tf_op jit(solution)/shard_map/analyse/pallas_call | solution.py:219
  35.7 18.8 %all_to_all.11 = bf16[32,6,8,128]{3,2,1,0:T(8,128)(2,1)S(1)} all-to-all(bf16[32,6,8,128]{3,2,1,0:T(8,128)(2,1)S(1)} %analyse.1), channel_id=1, replica_groups={{432,416,400,384,368,352,336,320,304,288,272,256,240,224,208,192,176,16..., dimensions={0} | all-to-all | bytes 786432 | tf_op jit(solution)/shard_map/all_to_all | solution.py:227
  54.5 0.8 %copy.7 = bf16[8,32,6,128]{3,1,2,0:T(8,128)(2,1)} copy(bf16[8,32,6,128]{3,0,2,1:T(8,128)(2,1)S(1)} %bitcast.9) | data formatting | bytes 786432 | tf_op jit(solution)/shard_map/transpose | solution.py:228
  (2 shorter events, 0.0 us)
Async XLA Ops:
  0.8 4.6 %copy-start.4 = (s32[32,4]{0,1:T(4,128)S(1)}, s32[32,4]{0,1:T(4,128)}, u32[]{:S(2)}) copy-start(s32[32,4]{0,1:T(4,128)} %param.10) | copy-start | bytes 1540
  0.8 4.6 %copy-start = (bf16[8,32,6,128]{3,1,2,0:T(8,128)(2,1)S(1)}, bf16[8,32,6,128]{3,1,2,0:T(8,128)(2,1)}, u32[]{:S(2)}) copy-start(bf16[8,32,6,128]{3,1,2,0:T(8,128)(2,1)} %param.6) | copy-start | bytes 1179652
  0.8 4.6 %copy-start.1 = (bf16[8,32,128]{2,1,0:T(8,128)(2,1)S(1)}, bf16[8,32,128]{2,1,0:T(8,128)(2,1)}, u32[]{:S(2)}) copy-start(bf16[8,32,128]{2,1,0:T(8,128)(2,1)} %anomalies_ref.1) | copy-start | bytes 196612
  0.8 4.6 %copy-start.2 = (f32[32,4,128]{2,1,0:T(4,128)S(1)}, f32[32,4,128]{2,1,0:T(4,128)}, u32[]{:S(2)}) copy-start(f32[32,4,128]{2,1,0:T(4,128)} %loc_ref.1) | copy-start | bytes 196612
  0.8 5.7 %collective-permute-start = (bf16[9,3,128]{2,1,0:T(4,128)(2,1)S(1)}, bf16[9,3,128]{2,1,0:T(4,128)(2,1)S(1)}, u32[]{:S(2)}, u32[]{:S(2)}) collective-permute-start(bf16[9,3,128]{2,1,0:T(4,128)(2,1)S(1)} %get-tuple-element.17), channel_id=1, source_target_pairs={{0,1},{1,2},{2,3},{3,4},{4,5},{5,6},{6,7},{7,8},{8,9},{9,10},{10,1... | collective-permute-start | bytes 20744 | tf_op jit(solution)/shard_map/ppermute | solution.py:182
  4.7 4.3 %collective-permute-start.1 = (bf16[9,3,128]{2,1,0:T(4,128)(2,1)S(1)}, bf16[9,3,128]{2,1,0:T(4,128)(2,1)S(1)}, u32[]{:S(2)}, u32[]{:S(2)}) collective-permute-start(bf16[9,3,128]{2,1,0:T(4,128)(2,1)S(1)} %get-tuple-element.18), channel_id=1, source_target_pairs={{1,0},{2,1},{3,2},{4,3},{5,4},{6,5},{7,6},{8,7},{9,8},{10,9},{11,1... | collective-permute-start | bytes 20744 | tf_op jit(solution)/shard_map/ppermute | solution.py:183
  5.4 0.7 %copy-start.3 = (bf16[32,128]{1,0:T(8,128)(2,1)S(1)}, bf16[32,128]{1,0:T(8,128)(2,1)}, u32[]{:S(2)}) copy-start(bf16[32,128]{1,0:T(8,128)(2,1)} %misfit_ref.1) | copy-start | bytes 24580

commit v9 on v8

--- a/solution.py
+++ b/solution.py
@@ -181,9 +181,9 @@
     )(stacked[:, count - HW :], stacked[:, :HW])
     before = lax.ppermute(tail, "region", up)
     after = lax.ppermute(head, "region", [(j, i) for i, j in up])
-    order = [(27 - i) % ranks for i in range(ranks)]
+    order = [(25 - i) % ranks for i in range(ranks)]
     me = lax.axis_index("member").reshape(1)
-    me = (27 - me + ranks) % ranks
+    me = (25 - me + ranks) % ranks
     table = jnp.concatenate([table, jnp.broadcast_to(tally[None], (1, slots))], axis=0)
     blocks = jax.ShapeDtypeStruct((slots, used, members, obs), anomalies.dtype)
     rows = jax.ShapeDtypeStruct((8, used * obs), jnp.float32)

time: 55.7 us -> 55.5 us (level)
  the two profiles are of different devices: /device:TPU:193 before, /device:TPU:199 now
where the time goes in v9:
time: 55.5 us; the launch traced here: 55.2 us
  blocking collectives  42.8 us (77%)
  starting transfers between devices  3.88 us (7%)
  Pallas kernels  2.93 us (5%)
  waiting for transfers between devices  2.5 us (5%)
  local copies, waits for them, and re-layouts  1.51 us (3%)
  other arithmetic  0.78 us (1%)
  between operations  0.78 us (1%)
    all_to_all x1, blocking collectives, shards(): lax.all_to_all(outgoing, 'member', 0, 0, tiled=True, axis_index_groups=[o...  23.8 us
    all_to_all x1, blocking collectives, shards(): lax.all_to_all(back, 'member', 0, 0, tiled=True, axis_index_groups=[order])  19 us
    ppermute x1, starting transfers between devices, shards(): before = lax.ppermute(tail, 'region', up)  3.88 us
    ppermute x1, waiting for transfers between devices, shards(): after = lax.ppermute(head, 'region', [(j, i) for i, j in up])  2.5 us
    pallas_call x1, Pallas kernels, shards(): pl.pallas_call(functools.partial(analyse_kernel, fields), out_shape=jax.S...  2.25 us
  transfers between devices with their start and end apart: 2, of which 1 were waited for; matrix products, arithmetic and copies ran while one was open for 0% of the time, Pallas kernels for 1%

profile of v9, /device:TPU:199, one launch (start us, length us, event | category | flops | bytes accessed | tf_op | source)
XLA Modules:
  0.0 55.2 jit_solution(7667755941634919957)
XLA Ops:
  0.0 0.8 %pad_maximum_fusion = (bf16[9,3,128]{2,1,0:T(4,128)(2,1)S(1)}, bf16[9,3,128]{2,1,0:T(4,128)(2,1)S(1)}) fusion(bf16[1,32,128]{2,1,0:T(8,128)(2,1)} %bitcast.8, bf16[8,32,128]{2,1,0:T(8,128)(2,1)} %anomalies_ref.1), kind=kLoop, calls=%fused_computation | loop fusion | flops 27648 | bytes 87552 | tf_op jit(solution)/shard_map/concatenate | solution.py:170
  0.8 0.0 copy-start.4
  0.8 0.0 copy-start
  0.8 0.0 copy-start.1
  0.8 0.0 copy-start.2
  0.8 3.9 %collective-permute-start = (bf16[9,3,128]{2,1,0:T(4,128)(2,1)S(1)}, bf16[9,3,128]{2,1,0:T(4,128)(2,1)S(1)}, u32[]{:S(2)}, u32[]{:S(2)}) collective-permute-start(bf16[9,3,128]{2,1,0:T(4,128)(2,1)S(1)} %get-tuple-element.17), channel_id=1, source_target_pairs={{0,1},{1,2},{2,3},{3,4},{4,5},{5,6},{6,7},{7,8},{8,9},{9,10},{10,1... | collective-permute-start | bytes 20744 | tf_op jit(solution)/shard_map/ppermute | solution.py:182
  4.7 0.0 collective-permute-start.1
  5.4 0.0 copy-start.3
  5.4 0.0 copy-done.4
  5.4 0.0 copy-done
  5.4 0.0 copy-done.1
  5.4 0.0 copy-done.2
  5.5 0.6 %copy-done.3 = bf16[32,128]{1,0:T(8,128)(2,1)S(1)} copy-done((bf16[32,128]{1,0:T(8,128)(2,1)S(1)}, bf16[32,128]{1,0:T(8,128)(2,1)}, u32[]{:S(2)}) %copy-start.3) | copy-done | bytes 8216
  6.1 0.4 pack.1
  6.5 0.0 collective-permute-done.before_ref
  6.5 2.5 %collective-permute-done.1.after_ref = bf16[9,3,128]{2,1,0:T(4,128)(2,1)S(1)} collective-permute-done((bf16[9,3,128]{2,1,0:T(4,128)(2,1)S(1)}, bf16[9,3,128]{2,1,0:T(4,128)(2,1)S(1)}, u32[]{:S(2)}, u32[]{:S(2)}) %collective-permute-start.1) | collective-permute-done | bytes 6944 | tf_op jit(solution)/shard_map/ppermute | solution.py:183
  9.0 0.2 choose.1
  9.3 23.8 %all_to_all.10.incoming_ref = bf16[32,10,8,128]{3,2,1,0:T(8,128)(2,1)S(1)} all-to-all(bf16[32,10,8,128]{3,2,1,0:T(8,128)(2,1)S(1)} %get-tuple-element.19), channel_id=1, replica_groups={{400,384,368,352,336,320,304,288,272,256,240,224,208,192,176,160,144,12..., dimensions={0} | all-to-all | bytes 1310720 | tf_op jit(solution)/shard_map/all_to_all | solution.py:218
  33.1 2.2 %analyse.1 = bf16[32,6,8,128]{3,2,1,0:T(8,128)(2,1)S(1)} custom-call(bf16[32,10,8,128]{3,2,1,0:T(8,128)(2,1)S(1)} %all_to_all.10.incoming_ref, f32[8,512]{1,0:T(8,128)S(1)} %get-tuple-element.20.side_ref), custom_call_target="tpu_custom_call" | custom-call | tf_op jit(solution)/shard_map/analyse/pallas_call | solution.py:219
  35.3 19.0 %all_to_all.11 = bf16[32,6,8,128]{3,2,1,0:T(8,128)(2,1)S(1)} all-to-all(bf16[32,6,8,128]{3,2,1,0:T(8,128)(2,1)S(1)} %analyse.1), channel_id=1, replica_groups={{400,384,368,352,336,320,304,288,272,256,240,224,208,192,176,160,144,12..., dimensions={0} | all-to-all | bytes 786432 | tf_op jit(solution)/shard_map/all_to_all | solution.py:227
  54.4 0.8 %copy.7 = bf16[8,32,6,128]{3,1,2,0:T(8,128)(2,1)} copy(bf16[8,32,6,128]{3,0,2,1:T(8,128)(2,1)S(1)} %bitcast.9) | data formatting | bytes 786432 | tf_op jit(solution)/shard_map/transpose | solution.py:228
  (2 shorter events, 0.0 us)
Async XLA Ops:
  0.8 4.6 %copy-start.4 = (s32[32,4]{0,1:T(4,128)S(1)}, s32[32,4]{0,1:T(4,128)}, u32[]{:S(2)}) copy-start(s32[32,4]{0,1:T(4,128)} %param.10) | copy-start | bytes 1540
  0.8 4.6 %copy-start = (bf16[8,32,6,128]{3,1,2,0:T(8,128)(2,1)S(1)}, bf16[8,32,6,128]{3,1,2,0:T(8,128)(2,1)}, u32[]{:S(2)}) copy-start(bf16[8,32,6,128]{3,1,2,0:T(8,128)(2,1)} %param.6) | copy-start | bytes 1179652
  0.8 4.6 %copy-start.1 = (bf16[8,32,128]{2,1,0:T(8,128)(2,1)S(1)}, bf16[8,32,128]{2,1,0:T(8,128)(2,1)}, u32[]{:S(2)}) copy-start(bf16[8,32,128]{2,1,0:T(8,128)(2,1)} %anomalies_ref.1) | copy-start | bytes 196612
  0.8 4.6 %copy-start.2 = (f32[32,4,128]{2,1,0:T(4,128)S(1)}, f32[32,4,128]{2,1,0:T(4,128)}, u32[]{:S(2)}) copy-start(f32[32,4,128]{2,1,0:T(4,128)} %loc_ref.1) | copy-start | bytes 196612
  0.8 5.7 %collective-permute-start = (bf16[9,3,128]{2,1,0:T(4,128)(2,1)S(1)}, bf16[9,3,128]{2,1,0:T(4,128)(2,1)S(1)}, u32[]{:S(2)}, u32[]{:S(2)}) collective-permute-start(bf16[9,3,128]{2,1,0:T(4,128)(2,1)S(1)} %get-tuple-element.17), channel_id=1, source_target_pairs={{0,1},{1,2},{2,3},{3,4},{4,5},{5,6},{6,7},{7,8},{8,9},{9,10},{10,1... | collective-permute-start | bytes 20744 | tf_op jit(solution)/shard_map/ppermute | solution.py:182
  4.7 4.3 %collective-permute-start.1 = (bf16[9,3,128]{2,1,0:T(4,128)(2,1)S(1)}, bf16[9,3,128]{2,1,0:T(4,128)(2,1)S(1)}, u32[]{:S(2)}, u32[]{:S(2)}) collective-permute-start(bf16[9,3,128]{2,1,0:T(4,128)(2,1)S(1)} %get-tuple-element.18), channel_id=1, source_target_pairs={{1,0},{2,1},{3,2},{4,3},{5,4},{6,5},{7,6},{8,7},{9,8},{10,9},{11,1... | collective-permute-start | bytes 20744 | tf_op jit(solution)/shard_map/ppermute | solution.py:183
  5.4 0.7 %copy-start.3 = (bf16[32,128]{1,0:T(8,128)(2,1)S(1)}, bf16[32,128]{1,0:T(8,128)(2,1)}, u32[]{:S(2)}) copy-start(bf16[32,128]{1,0:T(8,128)(2,1)} %misfit_ref.1) | copy-start | bytes 24580

commit v10 on v9

--- a/solution.py
+++ b/solution.py
@@ -181,9 +181,9 @@
     )(stacked[:, count - HW :], stacked[:, :HW])
     before = lax.ppermute(tail, "region", up)
     after = lax.ppermute(head, "region", [(j, i) for i, j in up])
-    order = [(25 - i) % ranks for i in range(ranks)]
+    order = [(19 - i) % ranks for i in range(ranks)]
     me = lax.axis_index("member").reshape(1)
-    me = (25 - me + ranks) % ranks
+    me = (19 - me + ranks) % ranks
     table = jnp.concatenate([table, jnp.broadcast_to(tally[None], (1, slots))], axis=0)
     blocks = jax.ShapeDtypeStruct((slots, used, members, obs), anomalies.dtype)
     rows = jax.ShapeDtypeStruct((8, used * obs), jnp.float32)

time: 55.5 us -> 55.7 us (level)
  the two profiles are of different devices: /device:TPU:199 before, /device:TPU:193 now
where the time goes in v10:
time: 55.7 us; the launch traced here: 55.5 us
  blocking collectives  43.1 us (77%)
  starting transfers between devices  3.88 us (7%)
  Pallas kernels  2.93 us (5%)
  waiting for transfers between devices  2.5 us (4%)
  local copies, waits for them, and re-layouts  1.51 us (3%)
  other arithmetic  0.78 us (1%)
  between operations  0.78 us (1%)
    all_to_all x1, blocking collectives, shards(): lax.all_to_all(outgoing, 'member', 0, 0, tiled=True, axis_index_groups=[o...  24 us
    all_to_all x1, blocking collectives, shards(): lax.all_to_all(back, 'member', 0, 0, tiled=True, axis_index_groups=[order])  19.1 us
    ppermute x1, starting transfers between devices, shards(): before = lax.ppermute(tail, 'region', up)  3.88 us
    ppermute x1, waiting for transfers between devices, shards(): after = lax.ppermute(head, 'region', [(j, i) for i, j in up])  2.5 us
    pallas_call x1, Pallas kernels, shards(): pl.pallas_call(functools.partial(analyse_kernel, fields), out_shape=jax.S...  2.25 us
  transfers between devices with their start and end apart: 2, of which 1 were waited for; matrix products, arithmetic and copies ran while one was open for 0% of the time, Pallas kernels for 1%

profile of v10, /device:TPU:193, one launch (start us, length us, event | category | flops | bytes accessed | tf_op | source)
XLA Modules:
  0.0 55.5 jit_solution(8099413938901149990)
XLA Ops:
  0.0 0.8 %pad_maximum_fusion = (bf16[9,3,128]{2,1,0:T(4,128)(2,1)S(1)}, bf16[9,3,128]{2,1,0:T(4,128)(2,1)S(1)}) fusion(bf16[1,32,128]{2,1,0:T(8,128)(2,1)} %bitcast.8, bf16[8,32,128]{2,1,0:T(8,128)(2,1)} %anomalies_ref.1), kind=kLoop, calls=%fused_computation | loop fusion | flops 27648 | bytes 87552 | tf_op jit(solution)/shard_map/concatenate | solution.py:170
  0.8 0.0 copy-start.4
  0.8 0.0 copy-start
  0.8 0.0 copy-start.1
  0.8 0.0 copy-start.2
  0.8 3.9 %collective-permute-start = (bf16[9,3,128]{2,1,0:T(4,128)(2,1)S(1)}, bf16[9,3,128]{2,1,0:T(4,128)(2,1)S(1)}, u32[]{:S(2)}, u32[]{:S(2)}) collective-permute-start(bf16[9,3,128]{2,1,0:T(4,128)(2,1)S(1)} %get-tuple-element.17), channel_id=1, source_target_pairs={{0,1},{1,2},{2,3},{3,4},{4,5},{5,6},{6,7},{7,8},{8,9},{9,10},{10,1... | collective-permute-start | bytes 20744 | tf_op jit(solution)/shard_map/ppermute | solution.py:182
  4.7 0.0 collective-permute-start.1
  5.4 0.0 copy-start.3
  5.4 0.0 copy-done.4
  5.4 0.0 copy-done
  5.4 0.0 copy-done.1
  5.4 0.0 copy-done.2
  5.5 0.6 %copy-done.3 = bf16[32,128]{1,0:T(8,128)(2,1)S(1)} copy-done((bf16[32,128]{1,0:T(8,128)(2,1)S(1)}, bf16[32,128]{1,0:T(8,128)(2,1)}, u32[]{:S(2)}) %copy-start.3) | copy-done | bytes 8216
  6.1 0.4 pack.1
  6.5 0.0 collective-permute-done.before_ref
  6.5 2.5 %collective-permute-done.1.after_ref = bf16[9,3,128]{2,1,0:T(4,128)(2,1)S(1)} collective-permute-done((bf16[9,3,128]{2,1,0:T(4,128)(2,1)S(1)}, bf16[9,3,128]{2,1,0:T(4,128)(2,1)S(1)}, u32[]{:S(2)}, u32[]{:S(2)}) %collective-permute-start.1) | collective-permute-done | bytes 6944 | tf_op jit(solution)/shard_map/ppermute | solution.py:183
  9.0 0.2 choose.1
  9.3 24.0 %all_to_all.10.incoming_ref = bf16[32,10,8,128]{3,2,1,0:T(8,128)(2,1)S(1)} all-to-all(bf16[32,10,8,128]{3,2,1,0:T(8,128)(2,1)S(1)} %get-tuple-element.19), channel_id=1, replica_groups={{304,288,272,256,240,224,208,192,176,160,144,128,112,96,80,64,48,32,16,..., dimensions={0} | all-to-all | bytes 1310720 | tf_op jit(solution)/shard_map/all_to_all | solution.py:218
  33.3 2.2 %analyse.1 = bf16[32,6,8,128]{3,2,1,0:T(8,128)(2,1)S(1)} custom-call(bf16[32,10,8,128]{3,2,1,0:T(8,128)(2,1)S(1)} %all_to_all.10.incoming_ref, f32[8,512]{1,0:T(8,128)S(1)} %get-tuple-element.20.side_ref), custom_call_target="tpu_custom_call" | custom-call | tf_op jit(solution)/shard_map/analyse/pallas_call | solution.py:219
  35.5 19.1 %all_to_all.11 = bf16[32,6,8,128]{3,2,1,0:T(8,128)(2,1)S(1)} all-to-all(bf16[32,6,8,128]{3,2,1,0:T(8,128)(2,1)S(1)} %analyse.1), channel_id=1, replica_groups={{304,288,272,256,240,224,208,192,176,160,144,128,112,96,80,64,48,32,16,..., dimensions={0} | all-to-all | bytes 786432 | tf_op jit(solution)/shard_map/all_to_all | solution.py:227
  54.6 0.8 %copy.7 = bf16[8,32,6,128]{3,1,2,0:T(8,128)(2,1)} copy(bf16[8,32,6,128]{3,0,2,1:T(8,128)(2,1)S(1)} %bitcast.9) | data formatting | bytes 786432 | tf_op jit(solution)/shard_map/transpose | solution.py:228
  (2 shorter events, 0.0 us)
Async XLA Ops:
  0.8 4.6 %copy-start.4 = (s32[32,4]{0,1:T(4,128)S(1)}, s32[32,4]{0,1:T(4,128)}, u32[]{:S(2)}) copy-start(s32[32,4]{0,1:T(4,128)} %param.10) | copy-start | bytes 1540
  0.8 4.6 %copy-start = (bf16[8,32,6,128]{3,1,2,0:T(8,128)(2,1)S(1)}, bf16[8,32,6,128]{3,1,2,0:T(8,128)(2,1)}, u32[]{:S(2)}) copy-start(bf16[8,32,6,128]{3,1,2,0:T(8,128)(2,1)} %param.6) | copy-start | bytes 1179652
  0.8 4.6 %copy-start.1 = (bf16[8,32,128]{2,1,0:T(8,128)(2,1)S(1)}, bf16[8,32,128]{2,1,0:T(8,128)(2,1)}, u32[]{:S(2)}) copy-start(bf16[8,32,128]{2,1,0:T(8,128)(2,1)} %anomalies_ref.1) | copy-start | bytes 196612
  0.8 4.6 %copy-start.2 = (f32[32,4,128]{2,1,0:T(4,128)S(1)}, f32[32,4,128]{2,1,0:T(4,128)}, u32[]{:S(2)}) copy-start(f32[32,4,128]{2,1,0:T(4,128)} %loc_ref.1) | copy-start | bytes 196612
  0.8 5.7 %collective-permute-start = (bf16[9,3,128]{2,1,0:T(4,128)(2,1)S(1)}, bf16[9,3,128]{2,1,0:T(4,128)(2,1)S(1)}, u32[]{:S(2)}, u32[]{:S(2)}) collective-permute-start(bf16[9,3,128]{2,1,0:T(4,128)(2,1)S(1)} %get-tuple-element.17), channel_id=1, source_target_pairs={{0,1},{1,2},{2,3},{3,4},{4,5},{5,6},{6,7},{7,8},{8,9},{9,10},{10,1... | collective-permute-start | bytes 20744 | tf_op jit(solution)/shard_map/ppermute | solution.py:182
  4.7 4.3 %collective-permute-start.1 = (bf16[9,3,128]{2,1,0:T(4,128)(2,1)S(1)}, bf16[9,3,128]{2,1,0:T(4,128)(2,1)S(1)}, u32[]{:S(2)}, u32[]{:S(2)}) collective-permute-start(bf16[9,3,128]{2,1,0:T(4,128)(2,1)S(1)} %get-tuple-element.18), channel_id=1, source_target_pairs={{1,0},{2,1},{3,2},{4,3},{5,4},{6,5},{7,6},{8,7},{9,8},{10,9},{11,1... | collective-permute-start | bytes 20744 | tf_op jit(solution)/shard_map/ppermute | solution.py:183
  5.4 0.7 %copy-start.3 = (bf16[32,128]{1,0:T(8,128)(2,1)S(1)}, bf16[32,128]{1,0:T(8,128)(2,1)}, u32[]{:S(2)}) copy-start(bf16[32,128]{1,0:T(8,128)(2,1)} %misfit_ref.1) | copy-start | bytes 24580
